TPU v7x, 32 devices: a whole 2x2x4 slice. The times are simulated.
32 devices in a mesh: band: 16 (over z, x, core), lev: 2 (over y).
Axes of the slice: x: 2, y: 2, z: 4, core: 2. Of those that a mesh axis runs over, the one named last changes fastest.
Arguments:
- obs_vals: bfloat16 [2, 24, 16384], P('lev', None, 'band'), may hold values from -400 to 400
- obs_colat: bfloat16 [16384], P('band'), may hold values from -1 to 1
- obs_lon: int32 [16384], P('band'), may hold values from 0 to 511
- band_list: int32 [16, 16, 128], P('band'), may hold values from 0 to 1023, as said below
- counts: int32 [16, 16], P('band'), may hold values from 0 to 128, as said below
- w_in: bfloat16 [48, 256], replicated, may hold values from -0.875 to 0.875
- b_in: float32 [256], replicated, may hold values from -3 to 3
- w_out: bfloat16 [256, 256], P(None, 'lev'), may hold values from -0.375 to 0.375
- b_out: float32 [256], P('lev'), may hold values from -3 to 3
Outputs:
- encoded: bfloat16 [256, 512, 128], P('lev', 'band')
Inputs may be any that keep to these rules, and one draw needn't show every extreme that they name: For each device s and band b the first counts[s, b] entries of band_list[s, b] are indices (within device s) of observations in band b; over all b they name every observation of device s exactly once. Later entries are padding and name arbitrary observations. `counts`: each row sums to 1024. Some band receives 128 observations from every device.
All inputs are finite; a program needn't handle non-finite values.
Results may differ from a plain program's by a relative error of at most 0.0063.
Values may be sent and summed in bfloat16 or wider, within the bound.
No kernel may reach another device: no remote copies, remote signals or barrier semaphores. Data moves between devices by JAX's collectives and lax.ppermute only.
A program may use at most 64 MiB of HBM per device.

v0:
```python
import math

import jax
import jax.numpy as jnp
from jax import lax
from jax.sharding import PartitionSpec as P

LAT_DEV = 8
LON_DEV = 32


norm_eps = 1e-05


def cheb_inverse(nodes):
    order_ids = jnp.arange(nodes, dtype=jnp.float32)[:, None]
    node_ids = jnp.arange(nodes, dtype=jnp.float32)[None, :]
    factor = jnp.where(order_ids == 0.0, 1.0, 2.0).astype(jnp.float32) / nodes
    return factor * jnp.cos(math.pi * order_ids * (node_ids + 0.5) / nodes)


def lat_weights(colat, nodes):
    angles = jnp.arccos(jnp.clip(colat, -1.0, 1.0))
    order_ids = jnp.arange(nodes, dtype=jnp.float32)
    cheb_terms = jnp.cos(order_ids[:, None] * angles[None, :])
    return jnp.dot(cheb_inverse(nodes).T, cheb_terms, precision=lax.Precision.HIGHEST)


def dct_table(length):
    mode_ids = jnp.arange(length, dtype=jnp.float32)[:, None]
    node_ids = jnp.arange(length, dtype=jnp.float32)[None, :]
    row_scale = jnp.where(mode_ids == 0.0, math.sqrt(1.0 / length), math.sqrt(2.0 / length)).astype(
        jnp.float32
    )
    return (row_scale * jnp.cos(math.pi * mode_ids * (node_ids + 0.5) / length)).astype(
        jnp.bfloat16
    )


def on_device(obs_vals, obs_colat, obs_lon, band_list, counts, w_in, b_in, w_out, b_out):
    band_count = lax.axis_size("band")
    capacity = band_list.shape[2]
    lat_nodes = LAT_DEV
    lon_local = LON_DEV
    lon_count = lon_local * band_count
    lat_total = lat_nodes * band_count
    channels = obs_vals.shape[1]
    feat_count = w_in.shape[0]
    picked = band_list[0].reshape(-1)
    live_slot = (jnp.arange(capacity, dtype=jnp.int32)[None, :] < counts[0][:, None]).reshape(-1)
    outgoing = jnp.where(
        live_slot[None, :], jnp.take(obs_vals[0], picked, axis=1), jnp.zeros((), jnp.bfloat16)
    )
    colat_out = jnp.take(obs_colat, picked)[None, :]
    lon_out = jnp.take(obs_lon, picked)[None, :]
    incoming, colat_in, lon_in = (
        lax.all_to_all(outgoing, "band", split_axis=1, concat_axis=1, tiled=True),
        lax.all_to_all(colat_out, "band", split_axis=1, concat_axis=1, tiled=True),
        lax.all_to_all(lon_out, "band", split_axis=1, concat_axis=1, tiled=True),
    )
    weights = lat_weights(colat_in[0].astype(jnp.float32), lat_nodes)
    weighted = (incoming.astype(jnp.float32)[:, None, :] * weights[None]).astype(jnp.bfloat16)
    weighted = weighted.reshape(channels * lat_nodes, -1)
    lon_ids = lon_in[0]
    row_count = weighted.shape[1]
    block_rows = math.gcd(row_count, 1024)
    columns = jnp.arange(lon_count, dtype=jnp.int32)

    def add_block(step_index, grid_sum):
        first_row = step_index * block_rows
        block_vals = lax.dynamic_slice_in_dim(weighted, first_row, block_rows, 1)
        block_lon = lax.dynamic_slice_in_dim(lon_ids, first_row, block_rows, 0)
        onehot = (block_lon[:, None] == columns[None, :]).astype(jnp.bfloat16)
        return grid_sum + jnp.dot(block_vals, onehot, preferred_element_type=jnp.float32)

    grid_sum = lax.fori_loop(
        0,
        row_count // block_rows,
        add_block,
        jnp.zeros((channels * lat_nodes, lon_count), jnp.float32),
    )
    grid_half = grid_sum.astype(jnp.bfloat16).reshape(channels, lat_nodes, lon_count)
    received = lax.all_to_all(grid_half, "band", split_axis=2, concat_axis=2, tiled=True)
    items = received.shape[0]
    arranged = received.reshape(items, lat_nodes, band_count, lon_local)
    table = dct_table(lat_total).reshape(lat_total, band_count, lat_nodes)
    spectrum = jnp.einsum(
        "cjbm,kbj->cmk", arranged, table, preferred_element_type=jnp.float32
    ).astype(jnp.bfloat16)
    shard_rows = lax.all_gather(spectrum, "lev", axis=0, tiled=True)
    pre_act = jnp.einsum("fh,fmk->hmk", w_in, shard_rows, preferred_element_type=jnp.float32)
    squared = shard_rows.astype(jnp.float32)
    pre_act, sum_sq = (pre_act, jnp.sum(squared * squared, axis=0))
    inv_norm = lax.rsqrt(sum_sq * (1.0 / feat_count) + norm_eps)
    hidden = jax.nn.gelu(pre_act * inv_norm[None] + b_in[:, None, None]).astype(jnp.bfloat16)
    output = (
        jnp.einsum("ho,hmk->omk", w_out, hidden, preferred_element_type=jnp.float32)
        + b_out[:, None, None]
    )
    return output.astype(jnp.bfloat16)


def solution(mesh):
    in_specs = (
        P("lev", None, "band"),
        P("band"),
        P("band"),
        P("band", None, None),
        P("band", None),
        P(),
        P(),
        P(None, "lev"),
        P("lev"),
    )
    out_specs = P("lev", "band", None)
    return jax.shard_map(
        on_device, mesh=mesh, in_specs=in_specs, out_specs=out_specs, check_vma=False
    )
```

profile of v0, /device:TPU:0, one launch (start us, length us, event | category | flops | bytes accessed | tf_op | source)
XLA Modules:
  0.0 93.2 jit_solution(5964530053610463450)
XLA Ops:
  0.0 0.8 compare_select_fusion
  0.8 13.1 %gather_fusion.1 = bf16[2048]{0:T(1024)(128)(2,1)S(1)} fusion(bf16[1024]{0:T(1024)(128)(2,1)S(1)} %copy-done.2, s32[2048]{0:T(1024)S(1)} %broadcast_clamp_fusion), kind=kCustom, calls=%fused_computation.1 | custom fusion | bytes 16384 | tf_op jit(solution)/shard_map/jit(_take)/gather | solution.py:54
  13.9 8.6 %gather_fusion.2 = s32[2048]{0:T(1024)S(1)} fusion(s32[1024]{0:T(1024)S(1)} %copy-done.1, s32[2048]{0:T(1024)S(1)} %broadcast_clamp_fusion), kind=kCustom, calls=%fused_computation.2 | custom fusion | bytes 24576 | tf_op jit(solution)/shard_map/jit(_take)/gather | solution.py:55
  22.5 0.6 bitcast_select_fusion
  23.1 0.6 copy.41
  23.7 7.4 %all-to-all-start.1 = ((bf16[1,16,128]{2,0,1:T(2,128)(2,1)}), bf16[1,16,128]{2,0,1:T(2,128)(2,1)S(1)}, u32[]{:S(2)}, u32[]{:S(2)}) async-start(bf16[1,16,128]{2,0,1:T(2,128)(2,1)} %copy.41), calls=%async_computation.1 | async-start | bytes 16384 | tf_op jit(solution)/shard_map/all_to_all | solution.py:58
  31.4 6.2 %gather_fusion = bf16[2048,24]{1,0:T(8,128)(2,1)S(1)} fusion(bf16[24,1024]{0,1:T(8,128)(2,1)S(1)} %bitcast.58, s32[2048]{0:T(1024)S(1)} %broadcast_clamp_fusion), kind=kCustom, calls=%fused_computation | custom fusion | bytes 204800 | tf_op jit(solution)/shard_map/jit(_take)/gather | solution.py:52
  37.8 0.7 select_select_fusion
  38.5 6.0 %all-to-all-start = ((bf16[24,16,128]{2,0,1:T(8,128)(2,1)}), bf16[24,16,128]{2,0,1:T(8,128)(2,1)S(1)}, u32[]{:S(2)}, u32[]{:S(2)}) async-start(bf16[24,16,128]{2,0,1:T(8,128)(2,1)} %select_select_fusion), calls=%async_computation | async-start | bytes 196608 | tf_op jit(solution)/shard_map/all_to_all | solution.py:57
  45.1 6.8 %all-to-all-done = bf16[24,16,128]{2,0,1:T(8,128)(2,1)S(1)} async-done(((bf16[24,16,128]{2,0,1:T(8,128)(2,1)}), bf16[24,16,128]{2,0,1:T(8,128)(2,1)S(1)}, u32[]{:S(2)}, u32[]{:S(2)}) %all-to-all-start) | async-done | bytes 98336 | tf_op jit(solution)/shard_map/all_to_all | solution.py:57
  51.9 3.5 %all-to-all-start.2 = ((s32[1,16,128]{2,0,1:T(1,128)}), s32[1,16,128]{2,0,1:T(1,128)S(1)}, u32[]{:S(2)}, u32[]{:S(2)}) async-start(s32[1,16,128]{2,0,1:T(1,128)} %bitcast.11), calls=%async_computation.2 | async-start | bytes 16384 | tf_op jit(solution)/shard_map/all_to_all | solution.py:59
  55.5 6.2 %all-to-all-done.2 = s32[1,16,128]{2,0,1:T(1,128)S(1)} async-done(((s32[1,16,128]{2,0,1:T(1,128)}), s32[1,16,128]{2,0,1:T(1,128)S(1)}, u32[]{:S(2)}, u32[]{:S(2)}) %all-to-all-start.2) | async-done | bytes 8224 | tf_op jit(solution)/shard_map/all_to_all | solution.py:59
  61.8 1.3 %while.14 = (s32[]{:T(128)}, f32[192,512]{1,0:T(8,128)S(1)}, bf16[192,2048]{1,0:T(8,128)(2,1)S(1)}, s32[2048]{0:T(1024)S(1)}, s32[]{:T(128)}, /*index=5*/s32[]{:T(128)}, s32[]{:T(128)}, s32[]{:T(128)}) while((s32[]{:T(128)}, f32[192,512]{1,0:T(8,128)S(1)}, bf16[192,2048]{1,0:T(8,128)(2,1)S(1)}, s32[2048]{0:T(1024)S(1)}, s32[]{:T(128)}, ...), condition=%wide.region_1.2_spmd.clone, body=%wide.region_0.1_spmd.clone.sunk | while | flops 202047488 | bytes 1192093 | solution.py:76
  61.8 0.6 fusion.54
  62.4 0.6 fusion.54
  63.1 0.8 copy.43
  64.0 2.0 %reshape.195 = bf16[16,2,3072]{2,1,0:T(2,128)(2,1)} reshape(bf16[512,8,24]{2,1,0:T(8,128)(2,1)S(1)} %bitcast.57) | data formatting | bytes 393216
  66.0 3.5 %all-to-all-start.3 = ((bf16[16,2,3072]{2,1,0:T(2,128)(2,1)}), bf16[16,2,3072]{2,1,0:T(2,128)(2,1)S(1)}, u32[]{:S(2)}, u32[]{:S(2)}) async-start(bf16[16,2,3072]{2,1,0:T(2,128)(2,1)} %reshape.195), calls=%async_computation.3 | async-start | bytes 393216 | tf_op jit(solution)/shard_map/all_to_all | solution.py:83
  69.5 8.9 %all-to-all-done.3 = bf16[16,2,3072]{2,1,0:T(2,128)(2,1)S(1)} async-done(((bf16[16,2,3072]{2,1,0:T(2,128)(2,1)}), bf16[16,2,3072]{2,1,0:T(2,128)(2,1)S(1)}, u32[]{:S(2)}, u32[]{:S(2)}) %all-to-all-start.3) | async-done | bytes 196640 | tf_op jit(solution)/shard_map/all_to_all | solution.py:83
  78.5 1.5 %reshape.196 = bf16[512,8,24]{2,1,0:T(8,128)(2,1)S(1)} reshape(bf16[16,2,3072]{2,1,0:T(2,128)(2,1)S(1)} %all-to-all-done.3) | data formatting | bytes 393216
  80.0 1.7 %copy.48 = bf16[24,8,16,32]{3,2,1,0:T(8,128)(2,1)S(1)} copy(bf16[24,8,16,32]{0,1,3,2:T(8,128)(2,1)S(1)} %bitcast.56) | data formatting | bytes 393216 | tf_op jit(solution)/shard_map/reshape | solution.py:85
  82.2 6.8 %all_gather.3 = bf16[48,32,128]{2,1,0:T(8,128)(2,1)S(1)} all-gather(bf16[24,32,128]{2,1,0:T(8,128)(2,1)S(1)} %fusion.17), channel_id=1, replica_groups=mesh['band'=16,'lev'=2] {'lev'}, dimensions={0}, use_global_device_ids=true | all-gather | bytes 589824 | tf_op jit(solution)/shard_map/all_gather | solution.py:90
  89.2 2.3 %fusion.16 = bf16[128,32,128]{0,2,1:T(8,128)(2,1)S(1)} fusion(f32[256]{0:T(256)S(1)} %copy-done.7, f32[32,128]{1,0:T(8,128)S(1)} %add_rsqrt_fusion, f32[128]{0:T(128)S(1)} %copy-done.8, bf16[48,32,128]{2,1,0:T(8,128)(2,1)S(1)} %all_gather.3, bf16[256,128]{1,0:T(8,128)(2,1)S(1)} %copy-done, bf16[48,256]{1,0:T(8,128)(2,1)S(1)} %copy-done.6), kind=kOutput, calls=%fused_computation.22 | convolution fusion | flops 381681664 | bytes 1549824 | tf_op jit(solution)/shard_map/ho,hmk->omk/dot_general | solution.py:97
  91.5 1.7 %copy.46 = bf16[128,32,128]{2,1,0:T(8,128)(2,1)} copy(bf16[128,32,128]{0,2,1:T(8,128)(2,1)S(1)} %fusion.16) | data formatting | bytes 2097152 | tf_op jit(solution)/shard_map/convert_element_type | solution.py:100
  (41 shorter events, 1.9 us)
Async XLA Ops:
  0.0 89.2 %copy-start = (bf16[256,128]{1,0:T(8,128)(2,1)S(1)}, bf16[256,128]{1,0:T(8,128)(2,1)}, u32[]{:S(2)}) copy-start(bf16[256,128]{1,0:T(8,128)(2,1)} %param.18) | copy-start | bytes 196612
  0.0 0.8 copy-start.2
  0.8 13.1 %copy-start.1 = (s32[1024]{0:T(1024)S(1)}, s32[1024]{0:T(1024)}, u32[]{:S(2)}) copy-start(s32[1024]{0:T(1024)} %param.13) | copy-start | bytes 12292
  13.9 8.6 %copy-start.3 = (s32[1,16,128]{2,1,0:T(8,128)S(1)}, s32[1,16,128]{2,1,0:T(8,128)}, u32[]{:S(2)}) copy-start(s32[1,16,128]{2,1,0:T(8,128)} %param.14) | copy-start | bytes 24580
  13.9 17.2 %copy-start.5 = (s32[1,16]{1,0:T(1,128)S(1)}, s32[1,16]{1,0:T(1,128)}, u32[]{:S(2)}) copy-start(s32[1,16]{1,0:T(1,128)} %param.15) | copy-start | bytes 196
  13.9 17.3 %copy-start.4 = (bf16[1,24,1024]{2,1,0:T(8,128)(2,1)S(1)}, bf16[1,24,1024]{2,1,0:T(8,128)(2,1)}, u32[]{:S(2)}) copy-start(bf16[1,24,1024]{2,1,0:T(8,128)(2,1)} %param.11) | copy-start | bytes 147460
  23.7 14.7 %all-to-all-start.1 = ((bf16[1,16,128]{2,0,1:T(2,128)(2,1)}), bf16[1,16,128]{2,0,1:T(2,128)(2,1)S(1)}, u32[]{:S(2)}, u32[]{:S(2)}) async-start(bf16[1,16,128]{2,0,1:T(2,128)(2,1)} %copy.41), calls=%async_computation.1 | async-start | bytes 16384 | tf_op jit(solution)/shard_map/all_to_all | solution.py:58
  38.5 13.4 %all-to-all-start = ((bf16[24,16,128]{2,0,1:T(8,128)(2,1)}), bf16[24,16,128]{2,0,1:T(8,128)(2,1)S(1)}, u32[]{:S(2)}, u32[]{:S(2)}) async-start(bf16[24,16,128]{2,0,1:T(8,128)(2,1)} %select_select_fusion), calls=%async_computation | async-start | bytes 196608 | tf_op jit(solution)/shard_map/all_to_all | solution.py:57
  51.9 9.9 %all-to-all-start.2 = ((s32[1,16,128]{2,0,1:T(1,128)}), s32[1,16,128]{2,0,1:T(1,128)S(1)}, u32[]{:S(2)}, u32[]{:S(2)}) async-start(s32[1,16,128]{2,0,1:T(1,128)} %bitcast.11), calls=%async_computation.2 | async-start | bytes 16384 | tf_op jit(solution)/shard_map/all_to_all | solution.py:59
  66.0 12.5 %all-to-all-start.3 = ((bf16[16,2,3072]{2,1,0:T(2,128)(2,1)}), bf16[16,2,3072]{2,1,0:T(2,128)(2,1)S(1)}, u32[]{:S(2)}, u32[]{:S(2)}) async-start(bf16[16,2,3072]{2,1,0:T(2,128)(2,1)} %reshape.195), calls=%async_computation.3 | async-start | bytes 393216 | tf_op jit(solution)/shard_map/all_to_all | solution.py:83
  81.7 7.5 %copy-start.6 = (bf16[48,256]{1,0:T(8,128)(2,1)S(1)}, bf16[48,256]{1,0:T(8,128)(2,1)}, u32[]{:S(2)}) copy-start(bf16[48,256]{1,0:T(8,128)(2,1)} %param.16) | copy-start | bytes 73732
  81.7 7.5 %copy-start.7 = (f32[256]{0:T(256)S(1)}, f32[256]{0:T(256)}, u32[]{:S(2)}) copy-start(f32[256]{0:T(256)} %param.17) | copy-start | bytes 3076
  81.7 7.5 %copy-start.8 = (f32[128]{0:T(128)S(1)}, f32[128]{0:T(128)}, u32[]{:S(2)}) copy-start(f32[128]{0:T(128)} %param.19) | copy-start | bytes 1540
where the time goes:
time: 93.7 us; the launch traced here: 93.2 us
  local copies, waits for them, and re-layouts  36.6 us (39%)
  waiting for transfers between devices  22 us (23%)
  starting transfers between devices  20.4 us (22%)
  blocking collectives  6.82 us (7%)
  matrix products  4.54 us (5%)
  other arithmetic  2.47 us (3%)
    gather x1, local copies, waits for them, and re-layouts, on_device(): colat_out = jnp.take(obs_colat, picked)[None, :]  13.1 us
    all_to_all x1, waiting for transfers between devices, on_device(): lax.all_to_all(grid_half, 'band', split_axis=2, concat_axis=2, tiled=True)  8.94 us
    gather x1, local copies, waits for them, and re-layouts, on_device(): lon_out = jnp.take(obs_lon, picked)[None, :]  8.58 us
    all_to_all x1, starting transfers between devices, on_device(): lax.all_to_all(colat_out, 'band', split_axis=1, concat_axis=1, tiled=True)  7.36 us
    all_to_all x1, waiting for transfers between devices, on_device(): lax.all_to_all(outgoing, 'band', split_axis=1, concat_axis=1, tiled=True)  6.84 us
    all_gather x1, blocking collectives, on_device(): shard_rows = lax.all_gather(spectrum, 'lev', axis=0, tiled=True)  6.82 us
    gather x2, local copies, waits for them, and re-layouts, on_device(): jnp.take(obs_vals[0], picked, axis=1)  6.38 us
    all_to_all x1, waiting for transfers between devices, on_device(): lax.all_to_all(lon_out, 'band', split_axis=1, concat_axis=1, tiled=True)  6.22 us
  transfers between devices with their start and end apart: 4, of which 3 were waited for; matrix products, arithmetic and copies ran while one was open for 9% of the time, Pallas kernels for 0%

commit v1 on v0

--- a/solution.py
+++ b/solution.py
@@ -3,13 +3,19 @@
 import jax
 import jax.numpy as jnp
 from jax import lax
+from jax.experimental import pallas as pl
+from jax.experimental.pallas import tpu as pltpu
 from jax.sharding import PartitionSpec as P
 
 LAT_DEV = 8
 LON_DEV = 32
-
+SUBS = 2
+ROWS = 32
+LANES = 128
 
 norm_eps = 1e-05
+bf16 = jnp.bfloat16
+f32 = jnp.float32
 
 
 def cheb_inverse(nodes):
@@ -37,7 +43,7 @@
     )
 
 
-def on_device(obs_vals, obs_colat, obs_lon, band_list, counts, w_in, b_in, w_out, b_out):
+def by_band(obs_vals, obs_colat, obs_lon, band_list, counts, w_in, b_in, w_out, b_out):
     band_count = lax.axis_size("band")
     capacity = band_list.shape[2]
     lat_nodes = LAT_DEV
@@ -100,6 +106,179 @@
     return output.astype(jnp.bfloat16)
 
 
+def onehot_dot(lhs, rhs, contract):
+    return lax.dot_general(lhs, rhs, (contract, ((), ())), preferred_element_type=f32)
+
+
+def iota(shape, dim):
+    return lax.broadcasted_iota(jnp.int32, shape, dim)
+
+
+def pack_kernel(bands, levels, odd_ref, counts_ref, list_ref, vals_ref, colat_ref, lon_ref, out_ref):
+    channels, obs = vals_ref.shape
+    blocks = obs // LANES
+    low_parts, high_parts = [], []
+    for band in range(bands):
+        entry = list_ref[band : band + 1, :]
+        live = iota((1, LANES), 1) < counts_ref[0, band]
+        entry = jnp.where(live, entry, -1)
+        high_parts.append(jnp.where((entry >> 7) == iota((blocks, LANES), 0), float(band), 0.0))
+        low_parts.append(jnp.where((entry & 127) == iota((LANES, LANES), 0), 1.0, 0.0))
+    high = jnp.concatenate(high_parts, axis=1).astype(bf16)
+    low = jnp.concatenate(low_parts, axis=1).astype(bf16)
+    band_of = onehot_dot(high, low, ((1,), (1,)))
+    band_row = jnp.concatenate([band_of[i : i + 1] for i in range(blocks)], axis=1)
+
+    lon = lon_ref[...]
+    sub_lons = LON_DEV // SUBS
+    cap = LANES // SUBS
+    groups = bands * SUBS
+    shift = sub_lons.bit_length() - 1
+    group = (lon >> shift) ^ odd_ref[0]
+    member = jnp.where(group == iota((groups, obs), 0), 1.0, 0.0)
+    upper = jnp.where(iota((LANES, LANES), 0) < iota((LANES, LANES), 1), 1.0, 0.0).astype(bf16)
+    carry = jnp.zeros((groups, 1), f32)
+    places = []
+    for i in range(blocks):
+        part = member[:, i * LANES : (i + 1) * LANES]
+        before = onehot_dot(part.astype(bf16), upper, ((1,), (0,))) + carry
+        places.append(jnp.sum(part * before, axis=0, keepdims=True))
+        carry = carry + jnp.sum(part, axis=1, keepdims=True)
+    place = jnp.concatenate(places, axis=1).astype(jnp.int32)
+    overflow = jnp.where(jnp.max(carry) > cap, 1.0, 0.0)
+    slot = jnp.where(place < cap, group * cap + place, -1)
+
+    meta = jnp.concatenate(
+        [
+            (lon & (LON_DEV - 1)).astype(f32),
+            band_row,
+            colat_ref[...].astype(f32),
+            jnp.zeros((ROWS - channels - 3, obs), f32),
+        ],
+        axis=0,
+    )
+    table = jnp.concatenate([vals_ref[...].astype(f32), meta], axis=0).astype(bf16)
+    flag_row = iota((ROWS, LANES), 0) == channels + 3
+    for dest in range(bands):
+        onehot = jnp.where(slot == iota((LANES, obs), 0) + dest * LANES, 1.0, 0.0).astype(bf16)
+        message = onehot_dot(table, onehot, ((1,), (1,)))
+        message = jnp.where(flag_row, overflow, message).astype(bf16)
+        for level in range(levels):
+            out_ref[level * bands + dest] = message
+
+
+def cheb_rows(colat):
+    nodes = LAT_DEV
+    x = jnp.broadcast_to(colat, (nodes, colat.shape[1]))
+    node = iota((nodes, 1), 0).astype(f32)
+    terms = [jnp.ones_like(x), x]
+    for _ in range(nodes - 2):
+        terms.append(2.0 * x * terms[-1] - terms[-2])
+    total = terms[0] * (1.0 / nodes)
+    for order in range(1, nodes):
+        scale = jnp.cos((math.pi * order / nodes) * (node + 0.5)) * (2.0 / nodes)
+        total = total + terms[order] * scale
+    return total
+
+
+def encode_kernel(
+    bands, levels, channels,
+    recv_ref, dct_ref, w_in_ref, b_in_ref, w_out_ref, b_out_ref, out_ref,
+    spec_ref, turn_ref,
+):
+    modes = LAT_DEV * bands
+    feats = levels * channels
+    sub_lons = LON_DEV // SUBS
+    slots = bands * (LANES // SUBS)
+    lower = iota((ROWS, LANES), 1) < LANES // SUBS
+
+    def half(level, sub):
+        pieces = []
+        for pair in range(bands // 2):
+            even = recv_ref[level * bands + 2 * pair]
+            odd = recv_ref[level * bands + 2 * pair + 1]
+            pieces.append(jnp.where(lower, even, odd) if sub == 0 else jnp.where(lower, odd, even))
+        return jnp.concatenate(pieces, axis=1)
+
+    for sub in range(SUBS):
+        parts = [half(level, sub) for level in range(levels)]
+        meta = parts[0][channels:].astype(f32)
+        values = jnp.concatenate([part[:channels] for part in parts], axis=0)
+        lon, band, colat = meta[0:1], meta[1:2], meta[2:3]
+        weight = cheb_rows(colat)
+        spread = jnp.concatenate(
+            [jnp.where(band == float(b), weight, 0.0) for b in range(bands)], axis=0
+        ).astype(bf16)
+        basis = onehot_dot(dct_ref[...], spread, ((1,), (0,))).astype(bf16)
+        for m in range(sub_lons):
+            here = jnp.where(lon == float(sub * sub_lons + m), 1.0, 0.0).astype(bf16)
+            mine = values * here
+            spec_ref[sub * sub_lons + m] = onehot_dot(mine, basis, ((1,), (1,))).astype(bf16)
+
+    w_first = w_in_ref[...].astype(f32).T.astype(bf16)
+    w_second = w_out_ref[...].astype(f32).T.astype(bf16)
+    b_first = jnp.broadcast_to(b_in_ref[...], (LANES, b_in_ref.shape[1])).T[:, :1]
+    b_second = jnp.broadcast_to(b_out_ref[...], (LANES, b_out_ref.shape[1])).T[:, :1]
+    out_rows = w_second.shape[0]
+    for m in range(LON_DEV):
+        spectrum = spec_ref[m]
+        wide = spectrum.astype(f32)
+        inv_norm = lax.rsqrt(
+            jnp.sum(wide * wide, axis=0, keepdims=True) * (1.0 / feats) + norm_eps
+        )
+        pre_act = onehot_dot(w_first, spectrum, ((1,), (0,)))
+        hidden = jax.nn.gelu(pre_act * inv_norm + b_first).astype(bf16)
+        encoded = onehot_dot(w_second, hidden, ((1,), (0,))) + b_second
+        for i in range(modes // LANES):
+            part = encoded[:, i * LANES : (i + 1) * LANES]
+            turn_ref[i, pl.ds(m, out_rows, stride=LON_DEV), :] = part
+    for i in range(modes // LANES):
+        turned = turn_ref[i].reshape(out_rows, LON_DEV, LANES).astype(bf16)
+        out_ref[:, :, i * LANES : (i + 1) * LANES] = turned
+
+
+def on_device(obs_vals, obs_colat, obs_lon, band_list, counts, w_in, b_in, w_out, b_out):
+    bands = lax.axis_size("band")
+    levels = lax.axis_size("lev")
+    channels = obs_vals.shape[1]
+    modes = LAT_DEV * bands
+    out_rows = w_out.shape[1]
+    vmem = pl.BlockSpec(memory_space=pltpu.VMEM)
+    smem = pl.BlockSpec(memory_space=pltpu.SMEM)
+    odd = (lax.axis_index("band") & 1).astype(jnp.int32).reshape(1)
+
+    packed = pl.pallas_call(
+        lambda *refs: pack_kernel(bands, levels, *refs),
+        out_shape=jax.ShapeDtypeStruct((levels * bands, ROWS, LANES), bf16),
+        in_specs=[smem, smem, vmem, vmem, vmem, vmem],
+        out_specs=vmem,
+        compiler_params=pltpu.CompilerParams(vmem_limit_bytes=48 << 20),
+        name="pack",
+    )(odd, counts, band_list[0], obs_vals[0], obs_colat.reshape(1, -1), obs_lon.reshape(1, -1))
+
+    received = lax.all_to_all(packed, ("lev", "band"), split_axis=0, concat_axis=0, tiled=True)
+    overflow = jnp.max(received[:, channels + 3, :].astype(f32)) > 0.0
+
+    def by_longitude():
+        return pl.pallas_call(
+            lambda *refs: encode_kernel(bands, levels, channels, *refs),
+            out_shape=jax.ShapeDtypeStruct((out_rows, LON_DEV, modes), bf16),
+            in_specs=[vmem] * 6,
+            out_specs=vmem,
+            scratch_shapes=[
+                pltpu.VMEM((LON_DEV, levels * channels, modes), bf16),
+                pltpu.VMEM((modes // LANES, out_rows * LON_DEV, LANES), f32),
+            ],
+            compiler_params=pltpu.CompilerParams(vmem_limit_bytes=48 << 20),
+            name="encode",
+        )(received, dct_table(modes), w_in, b_in.reshape(1, -1), w_out, b_out.reshape(1, -1))
+
+    def by_bands():
+        return by_band(obs_vals, obs_colat, obs_lon, band_list, counts, w_in, b_in, w_out, b_out)
+
+    return lax.cond(overflow, by_bands, by_longitude)
+
+
 def solution(mesh):
     in_specs = (
         P("lev", None, "band"),

time: 93.7 us -> 32.7 us (0.35)
  local copies, waits for them, and re-layouts: 36.6 us -> 1.65 us
  starting transfers between devices: 20.4 us -> 7.3 us
  waiting for transfers between devices: 22 us -> 10.3 us
  Pallas kernels: 0 us -> 11.3 us
  blocking collectives: 6.82 us -> 0 us
  matrix products: 4.54 us -> 0 us
  other arithmetic: 2.47 us -> 0.96 us
    gather x4 -> x0, local copies, waits for them, and re-layouts: 28 us -> none  [the longest x1 13.1 us: on_device(): colat_out = jnp.take(obs_colat, picked)[None, :]]
    all_to_all x4 -> x1, starting transfers between devices: 20.4 us -> 7.3 us  [on_device(): lax.all_to_all(packed, ('lev', 'band'), split_axis=0, concat_axis=0, tile...]
    all_to_all x4 -> x1, waiting for transfers between devices: 22 us -> 10.3 us  [on_device(): lax.all_to_all(packed, ('lev', 'band'), split_axis=0, concat_axis=0, tile...]
    pallas_call x0 -> x2, Pallas kernels: none -> 11.3 us  [the longest x1 7.88 us: by_longitude(): pl.pallas_call(lambda *refs: encode_kernel(bands, levels, channels, *refs...]
    all_gather x1 -> x0, blocking collectives: 6.82 us -> none  [on_device(): shard_rows = lax.all_gather(spectrum, 'lev', axis=0, tiled=True)]
    dot_general x5 -> x0, matrix products: 4.54 us -> none  [the longest x1 2.3 us: on_device(): jnp.einsum('ho,hmk->omk', w_out, hidden, preferred_element_type=jnp.float32)]
    unnamed x21 -> x2, local copies, waits for them, and re-layouts: 3.71 us -> 0.96 us
    select_n x4 -> x0, other arithmetic: 2.03 us -> none  [the longest x1 0.75 us: on_device(): jnp.take(obs_vals[0], picked, axis=1)]
  transfers between devices with their start and end apart: 4 -> 1, of which waited for: 3 -> 1; matrix products, arithmetic and copies ran while one was open for 9% -> 0% of each run, Pallas kernels for 0% -> 0%
where the time goes in v1:
time: 32.7 us; the launch traced here: 32.4 us
  Pallas kernels  11.3 us (35%)
  waiting for transfers between devices  10.3 us (31%)
  starting transfers between devices  7.3 us (22%)
  local copies, waits for them, and re-layouts  1.65 us (5%)
  other arithmetic  0.96 us (3%)
  between operations  0.68 us (2%)
    all_to_all x1, waiting for transfers between devices, on_device(): lax.all_to_all(packed, ('lev', 'band'), split_axis=0, concat_axis=0, tile...  10.3 us
    pallas_call x1, Pallas kernels, by_longitude(): pl.pallas_call(lambda *refs: encode_kernel(bands, levels, channels, *refs...  7.88 us
    all_to_all x1, starting transfers between devices, on_device(): lax.all_to_all(packed, ('lev', 'band'), split_axis=0, concat_axis=0, tile...  7.3 us
    pallas_call x1, Pallas kernels, on_device(): pl.pallas_call(lambda *refs: pack_kernel(bands, levels, *refs), out_shape...  3.41 us
    unnamed x2, local copies, waits for them, and re-layouts  0.96 us
    reshape x1, local copies, waits for them, and re-layouts, on_device(): obs_colat.reshape(1, -1)  0.69 us
  transfers between devices with their start and end apart: 1, of which 1 were waited for; matrix products, arithmetic and copies ran while one was open for 0% of the time, Pallas kernels for 0%

profile of v1, /device:TPU:0, one launch (start us, length us, event | category | flops | bytes accessed | tf_op | source)
XLA Modules:
  0.0 32.4 jit_solution(2845206170115144093)
XLA Ops:
  0.0 0.7 %reshape.198.refs_4_ = bf16[1,1024]{1,0:T(2,128)(2,1)S(1)} reshape(bf16[1024]{0:T(1024)(128)(2,1)} %param.14) | data formatting | bytes 4096 | tf_op jit(solution)/shard_map/reshape | solution.py:257
  0.7 3.4 %pack.1 = bf16[32,32,128]{2,1,0:T(8,128)(2,1)} custom-call(s32[1]{0:T(128)} %bitcast.24.refs_0_, s32[1,16]{1,0:T(1,128)} %refs_1_.1, s32[16,128]{1,0:T(8,128)} %bitcast.68, bf16[24,1024]{1,0:T(8,128)(2,1)} %bitcast.67, bf16[1,1024]{1,0:T(2,128)(2,1)S(1)} %reshape.198.refs_4_, s32[1,1024]{1,0:T(1,128)} %bitcast.62), custom_call_target="tpu_custom_call" | custom-call | tf_op jit(solution)/shard_map/pack/pallas_call | solution.py:250
  4.1 7.3 %all-to-all-start.4 = ((bf16[32,32,128]{2,1,0:T(8,128)(2,1)}), bf16[32,32,128]{2,1,0:T(8,128)(2,1)S(1)}, u32[]{:S(2)}, u32[]{:S(2)}) async-start(bf16[32,32,128]{2,1,0:T(8,128)(2,1)} %pack.1), calls=%async_computation.4 | async-start | bytes 524288 | tf_op jit(solution)/shard_map/all_to_all | solution.py:259
  11.4 10.3 %all-to-all-done.4 = bf16[32,32,128]{2,1,0:T(8,128)(2,1)S(1)} async-done(((bf16[32,32,128]{2,1,0:T(8,128)(2,1)}), bf16[32,32,128]{2,1,0:T(8,128)(2,1)S(1)}, u32[]{:S(2)}, u32[]{:S(2)}) %all-to-all-start.4) | async-done | bytes 262176 | tf_op jit(solution)/shard_map/all_to_all | solution.py:259
  21.7 0.6 %slice_reduce_fusion = bf16[]{:T(256)} fusion(bf16[32,32,128]{2,1,0:T(8,128)(2,1)S(1)} %all-to-all-done.4), kind=kLoop, calls=%fused_computation.82 | loop fusion | flops 4095 | bytes 8194 | tf_op jit(solution)/shard_map/reduce_max | solution.py:260
  23.0 8.5 %conditional.1 = (bf16[128,32,128]{2,1,0:T(8,128)(2,1)S(1)}) conditional(s32[]{:T(128)} %convert_element_type.57, (f32[256]{0:T(256)}, f32[128]{0:T(128)}, bf16[32,32,128]{2,1,0:T(8,128)(2,1)S(1)}, bf16[48,256]{1,0:T(8,128)(2,1)}, bf16[256,128]{1,0:T(8,128)(2,1)}) %tuple.25, (s32[1,16]{1,0:T(1,128)}, s32[1,16,128]{2,1,0:T(8,128)}, ...), branch_computations={%region_1.2_spmd, %region_2.6_spmd} | conditional | flops 612324352 | bytes 12258921 | solution.py:279
  23.0 0.3 multiply_convert_fusion.refs_1_
  23.3 7.9 %encode.1 = bf16[128,32,128]{2,1,0:T(8,128)(2,1)S(1)} custom-call(bf16[32,32,128]{2,1,0:T(8,128)(2,1)S(1)} %get-tuple-element.123.refs_0_, bf16[128,128]{1,0:T(8,128)(2,1)S(1)} %multiply_convert_fusion.refs_1_, bf16[48,256]{1,0:T(8,128)(2,1)} %get-tuple-element.124.refs_2_, f32[1,256]{1,0:T(1,128)} %bitcast.74, bf16[256,128]{1,0:T(8,128)(2,1)} %get-tuple-element.126.refs_4_, ...), custom_call_target="tpu_custom_call" | custom-call | tf_op jit(solution)/shard_map/cond/branch_0_fun/encode/pallas_call | solution.py:263
  31.5 0.0 copy-start.2
  31.5 1.0 %copy-done.2 = bf16[128,32,128]{2,1,0:T(8,128)(2,1)} copy-done((bf16[128,32,128]{2,1,0:T(8,128)(2,1)}, bf16[128,32,128]{2,1,0:T(8,128)(2,1)S(1)}, u32[]{:S(2)}) %copy-start.2) | copy-done | bytes 1048600
  (2 shorter events, 0.0 us)
Async XLA Ops:
  4.1 17.6 %all-to-all-start.4 = ((bf16[32,32,128]{2,1,0:T(8,128)(2,1)}), bf16[32,32,128]{2,1,0:T(8,128)(2,1)S(1)}, u32[]{:S(2)}, u32[]{:S(2)}) async-start(bf16[32,32,128]{2,1,0:T(8,128)(2,1)} %pack.1), calls=%async_computation.4 | async-start | bytes 524288 | tf_op jit(solution)/shard_map/all_to_all | solution.py:259
  31.5 1.0 %copy-start.2 = (bf16[128,32,128]{2,1,0:T(8,128)(2,1)}, bf16[128,32,128]{2,1,0:T(8,128)(2,1)S(1)}, u32[]{:S(2)}) copy-start(bf16[128,32,128]{2,1,0:T(8,128)(2,1)S(1)} %get-tuple-element.293) | copy-start | bytes 3145732

commit v2 on v1

--- a/solution.py
+++ b/solution.py
@@ -2,6 +2,8 @@
 
 import jax
 import jax.numpy as jnp
+import ml_dtypes
+import numpy as np
 from jax import lax
 from jax.experimental import pallas as pl
 from jax.experimental.pallas import tpu as pltpu
@@ -106,12 +108,28 @@
     return output.astype(jnp.bfloat16)
 
 
-def onehot_dot(lhs, rhs, contract):
+def table_const(length):
+    mode_ids = np.arange(length, dtype=np.float32)[:, None]
+    node_ids = np.arange(length, dtype=np.float32)[None, :]
+    scale = np.where(mode_ids == 0.0, math.sqrt(1.0 / length), math.sqrt(2.0 / length))
+    angle = np.float32(math.pi) * mode_ids * (node_ids + np.float32(0.5)) / np.float32(length)
+    return (scale.astype(np.float32) * np.cos(angle)).astype(ml_dtypes.bfloat16)
+
+
+def dot(lhs, rhs, contract):
     return lax.dot_general(lhs, rhs, (contract, ((), ())), preferred_element_type=f32)
 
 
 def iota(shape, dim):
     return lax.broadcasted_iota(jnp.int32, shape, dim)
+
+
+def one_where(mask):
+    return jnp.where(mask, 1.0, 0.0).astype(bf16)
+
+
+def row_of(tiles):
+    return jnp.concatenate([tiles[i : i + 1] for i in range(tiles.shape[0])], axis=1)
 
 
 def pack_kernel(bands, levels, odd_ref, counts_ref, list_ref, vals_ref, colat_ref, lon_ref, out_ref):
@@ -120,48 +138,60 @@
     low_parts, high_parts = [], []
     for band in range(bands):
         entry = list_ref[band : band + 1, :]
-        live = iota((1, LANES), 1) < counts_ref[0, band]
-        entry = jnp.where(live, entry, -1)
+        entry = jnp.where(iota((1, LANES), 1) < counts_ref[0, band], entry, -1)
         high_parts.append(jnp.where((entry >> 7) == iota((blocks, LANES), 0), float(band), 0.0))
-        low_parts.append(jnp.where((entry & 127) == iota((LANES, LANES), 0), 1.0, 0.0))
+        low_parts.append(one_where((entry & 127) == iota((LANES, LANES), 0)))
     high = jnp.concatenate(high_parts, axis=1).astype(bf16)
-    low = jnp.concatenate(low_parts, axis=1).astype(bf16)
-    band_of = onehot_dot(high, low, ((1,), (1,)))
-    band_row = jnp.concatenate([band_of[i : i + 1] for i in range(blocks)], axis=1)
-
-    lon = lon_ref[...]
+    low = jnp.concatenate(low_parts, axis=1)
+    band_row = row_of(dot(high, low, ((1,), (1,))))
+
+    lon = row_of(lon_ref[...])
     sub_lons = LON_DEV // SUBS
     cap = LANES // SUBS
     groups = bands * SUBS
-    shift = sub_lons.bit_length() - 1
-    group = (lon >> shift) ^ odd_ref[0]
+    group = (lon // sub_lons) ^ odd_ref[0]
     member = jnp.where(group == iota((groups, obs), 0), 1.0, 0.0)
-    upper = jnp.where(iota((LANES, LANES), 0) < iota((LANES, LANES), 1), 1.0, 0.0).astype(bf16)
+    earlier = one_where(iota((LANES, LANES), 0) < iota((LANES, LANES), 1))
     carry = jnp.zeros((groups, 1), f32)
     places = []
     for i in range(blocks):
         part = member[:, i * LANES : (i + 1) * LANES]
-        before = onehot_dot(part.astype(bf16), upper, ((1,), (0,))) + carry
+        before = dot(part.astype(bf16), earlier, ((1,), (0,))) + carry
         places.append(jnp.sum(part * before, axis=0, keepdims=True))
         carry = carry + jnp.sum(part, axis=1, keepdims=True)
     place = jnp.concatenate(places, axis=1).astype(jnp.int32)
     overflow = jnp.where(jnp.max(carry) > cap, 1.0, 0.0)
     slot = jnp.where(place < cap, group * cap + place, -1)
 
-    meta = jnp.concatenate(
+    depth = 2 * LANES
+    chunks = obs // depth
+    number = iota((1, obs), 1)
+    mine = (slot >> 7) == iota((bands, obs), 0)
+    held = jnp.where(mine, ((number & (depth - 1)) + 1).astype(f32), 0.0)
+    chunk = jnp.where(mine, (number // depth).astype(f32), 0.0)
+    lane = one_where((slot & (LANES - 1)) == iota((LANES, obs), 0))
+    found = dot(jnp.concatenate([held, chunk], axis=0).astype(bf16), lane, ((1,), (1,)))
+    held, chunk = row_of(found[:bands]), row_of(found[bands:])
+
+    rows = jnp.concatenate(
         [
+            vals_ref[...].astype(f32),
             (lon & (LON_DEV - 1)).astype(f32),
             band_row,
-            colat_ref[...].astype(f32),
+            row_of(colat_ref[...].astype(f32)),
             jnp.zeros((ROWS - channels - 3, obs), f32),
         ],
         axis=0,
-    )
-    table = jnp.concatenate([vals_ref[...].astype(f32), meta], axis=0).astype(bf16)
+    ).astype(bf16)
+    stacked = jnp.concatenate([rows[:, i * depth : (i + 1) * depth] for i in range(chunks)], axis=0)
+    pick = one_where(held == (iota((depth, bands * LANES), 0) + 1).astype(f32))
+    picked = dot(stacked, pick, ((1,), (0,)))
+    messages = jnp.zeros((ROWS, bands * LANES), f32)
+    for i in range(chunks):
+        messages = jnp.where(chunk == float(i), picked[i * ROWS : (i + 1) * ROWS], messages)
     flag_row = iota((ROWS, LANES), 0) == channels + 3
     for dest in range(bands):
-        onehot = jnp.where(slot == iota((LANES, obs), 0) + dest * LANES, 1.0, 0.0).astype(bf16)
-        message = onehot_dot(table, onehot, ((1,), (1,)))
+        message = messages[:, dest * LANES : (dest + 1) * LANES]
         message = jnp.where(flag_row, overflow, message).astype(bf16)
         for level in range(levels):
             out_ref[level * bands + dest] = message
@@ -171,26 +201,40 @@
     nodes = LAT_DEV
     x = jnp.broadcast_to(colat, (nodes, colat.shape[1]))
     node = iota((nodes, 1), 0).astype(f32)
-    terms = [jnp.ones_like(x), x]
-    for _ in range(nodes - 2):
-        terms.append(2.0 * x * terms[-1] - terms[-2])
-    total = terms[0] * (1.0 / nodes)
+    twice = x + x
+    before, now = jnp.ones_like(x), x
+    total = jnp.full_like(x, 1.0 / nodes)
     for order in range(1, nodes):
         scale = jnp.cos((math.pi * order / nodes) * (node + 0.5)) * (2.0 / nodes)
-        total = total + terms[order] * scale
+        total = total + now * scale
+        before, now = now, twice * now - before
     return total
+
+
+def gelu(x):
+    slope = math.sqrt(2.0 / math.pi)
+    half = 0.5 * x
+    return half + half * jnp.tanh(x * (slope + (0.044715 * slope) * (x * x)))
 
 
 def encode_kernel(
     bands, levels, channels,
     recv_ref, dct_ref, w_in_ref, b_in_ref, w_out_ref, b_out_ref, out_ref,
-    spec_ref, turn_ref,
+    spread_ref, spec_ref, turn_ref, done_ref, sems,
 ):
     modes = LAT_DEV * bands
     feats = levels * channels
     sub_lons = LON_DEV // SUBS
-    slots = bands * (LANES // SUBS)
     lower = iota((ROWS, LANES), 1) < LANES // SUBS
+    w_first = w_in_ref[...].astype(f32).T.astype(bf16)
+    w_second = w_out_ref[...].astype(f32).T.astype(bf16)
+    out_rows = w_second.shape[0]
+    batch = max(1, sub_lons * LANES // modes)
+    lane_tiles = batch * modes // LANES
+    b_first = jnp.broadcast_to(b_in_ref[...], (LANES, b_in_ref.shape[1])).T
+    b_second = jnp.broadcast_to(b_out_ref[...], (LANES, b_out_ref.shape[1])).T
+    b_first = jnp.concatenate([b_first] * lane_tiles, axis=1)
+    b_second = jnp.concatenate([b_second] * lane_tiles, axis=1)
 
     def half(level, sub):
         pieces = []
@@ -206,42 +250,56 @@
         values = jnp.concatenate([part[:channels] for part in parts], axis=0)
         lon, band, colat = meta[0:1], meta[1:2], meta[2:3]
         weight = cheb_rows(colat)
-        spread = jnp.concatenate(
+        nodes = jnp.concatenate(
             [jnp.where(band == float(b), weight, 0.0) for b in range(bands)], axis=0
         ).astype(bf16)
-        basis = onehot_dot(dct_ref[...], spread, ((1,), (0,))).astype(bf16)
+        basis = dot(dct_ref[...], nodes, ((1,), (0,))).astype(bf16)
+        spread = spread_ref.at[sub % spread_ref.shape[0]]
         for m in range(sub_lons):
-            here = jnp.where(lon == float(sub * sub_lons + m), 1.0, 0.0).astype(bf16)
-            mine = values * here
-            spec_ref[sub * sub_lons + m] = onehot_dot(mine, basis, ((1,), (1,))).astype(bf16)
-
-    w_first = w_in_ref[...].astype(f32).T.astype(bf16)
-    w_second = w_out_ref[...].astype(f32).T.astype(bf16)
-    b_first = jnp.broadcast_to(b_in_ref[...], (LANES, b_in_ref.shape[1])).T[:, :1]
-    b_second = jnp.broadcast_to(b_out_ref[...], (LANES, b_out_ref.shape[1])).T[:, :1]
-    out_rows = w_second.shape[0]
-    for m in range(LON_DEV):
-        spectrum = spec_ref[m]
-        wide = spectrum.astype(f32)
-        inv_norm = lax.rsqrt(
-            jnp.sum(wide * wide, axis=0, keepdims=True) * (1.0 / feats) + norm_eps
+            here = one_where(lon == float(sub * sub_lons + m))
+            spread[m * feats : (m + 1) * feats, :] = values * here
+        spec_ref[sub] = dot(spread[...], basis, ((1,), (1,))).astype(bf16)
+
+    copies = []
+    for sub in range(SUBS):
+        for first in range(0, sub_lons, batch):
+            spectrum = jnp.concatenate(
+                [spec_ref[sub, m * feats : (m + 1) * feats, :] for m in range(first, first + batch)],
+                axis=1,
+            )
+            wide = spectrum.astype(f32)
+            inv_norm = lax.rsqrt(
+                jnp.sum(wide * wide, axis=0, keepdims=True) * (1.0 / feats) + norm_eps
+            )
+            pre_act = dot(w_first, spectrum, ((1,), (0,)))
+            hidden = gelu(pre_act * inv_norm + b_first).astype(bf16)
+            encoded = dot(w_second, hidden, ((1,), (0,))) + b_second
+            for j in range(batch):
+                for i in range(modes // LANES):
+                    tile = j * (modes // LANES) + i
+                    turn_ref[sub, i, pl.ds(first + j, out_rows, stride=sub_lons), :] = encoded[
+                        :, tile * LANES : (tile + 1) * LANES
+                    ]
+        for i in range(modes // LANES):
+            turned = turn_ref[sub, i].reshape(out_rows, sub_lons, LANES).astype(bf16)
+            done_ref[sub, :, :, i * LANES : (i + 1) * LANES] = turned
+        copy = pltpu.make_async_copy(
+            done_ref.at[sub], out_ref.at[:, pl.ds(sub * sub_lons, sub_lons), :], sems.at[sub]
         )
-        pre_act = onehot_dot(w_first, spectrum, ((1,), (0,)))
-        hidden = jax.nn.gelu(pre_act * inv_norm + b_first).astype(bf16)
-        encoded = onehot_dot(w_second, hidden, ((1,), (0,))) + b_second
-        for i in range(modes // LANES):
-            part = encoded[:, i * LANES : (i + 1) * LANES]
-            turn_ref[i, pl.ds(m, out_rows, stride=LON_DEV), :] = part
-    for i in range(modes // LANES):
-        turned = turn_ref[i].reshape(out_rows, LON_DEV, LANES).astype(bf16)
-        out_ref[:, :, i * LANES : (i + 1) * LANES] = turned
+        copy.start()
+        copies.append(copy)
+    for copy in copies:
+        copy.wait()
 
 
 def on_device(obs_vals, obs_colat, obs_lon, band_list, counts, w_in, b_in, w_out, b_out):
     bands = lax.axis_size("band")
     levels = lax.axis_size("lev")
     channels = obs_vals.shape[1]
+    feats = levels * channels
     modes = LAT_DEV * bands
+    sub_lons = LON_DEV // SUBS
+    slots = bands * LANES // SUBS
     out_rows = w_out.shape[1]
     vmem = pl.BlockSpec(memory_space=pltpu.VMEM)
     smem = pl.BlockSpec(memory_space=pltpu.SMEM)
@@ -249,29 +307,36 @@
 
     packed = pl.pallas_call(
         lambda *refs: pack_kernel(bands, levels, *refs),
-        out_shape=jax.ShapeDtypeStruct((levels * bands, ROWS, LANES), bf16),
+        out_shape=pltpu.VMEM((levels * bands, ROWS, LANES), bf16),
         in_specs=[smem, smem, vmem, vmem, vmem, vmem],
         out_specs=vmem,
         compiler_params=pltpu.CompilerParams(vmem_limit_bytes=48 << 20),
         name="pack",
-    )(odd, counts, band_list[0], obs_vals[0], obs_colat.reshape(1, -1), obs_lon.reshape(1, -1))
+    )(
+        odd, counts, band_list[0], obs_vals[0],
+        obs_colat.reshape(-1, LANES), obs_lon.reshape(-1, LANES),
+    )
 
     received = lax.all_to_all(packed, ("lev", "band"), split_axis=0, concat_axis=0, tiled=True)
     overflow = jnp.max(received[:, channels + 3, :].astype(f32)) > 0.0
 
     def by_longitude():
+        spread_buffers = SUBS if bands <= 16 else 1
         return pl.pallas_call(
             lambda *refs: encode_kernel(bands, levels, channels, *refs),
             out_shape=jax.ShapeDtypeStruct((out_rows, LON_DEV, modes), bf16),
             in_specs=[vmem] * 6,
-            out_specs=vmem,
+            out_specs=pl.BlockSpec(memory_space=pltpu.HBM),
             scratch_shapes=[
-                pltpu.VMEM((LON_DEV, levels * channels, modes), bf16),
-                pltpu.VMEM((modes // LANES, out_rows * LON_DEV, LANES), f32),
+                pltpu.VMEM((spread_buffers, sub_lons * feats, slots), bf16),
+                pltpu.VMEM((SUBS, sub_lons * feats, modes), bf16),
+                pltpu.VMEM((SUBS, modes // LANES, out_rows * sub_lons, LANES), f32),
+                pltpu.VMEM((SUBS, out_rows, sub_lons, modes), bf16),
+                pltpu.SemaphoreType.DMA((SUBS,)),
             ],
-            compiler_params=pltpu.CompilerParams(vmem_limit_bytes=48 << 20),
+            compiler_params=pltpu.CompilerParams(vmem_limit_bytes=56 << 20),
             name="encode",
-        )(received, dct_table(modes), w_in, b_in.reshape(1, -1), w_out, b_out.reshape(1, -1))
+        )(received, table_const(modes), w_in, b_in.reshape(1, -1), w_out, b_out.reshape(1, -1))
 
     def by_bands():
         return by_band(obs_vals, obs_colat, obs_lon, band_list, counts, w_in, b_in, w_out, b_out)

time: 32.7 us -> 27.5 us (0.84)
  Pallas kernels: 11.3 us -> 7.09 us
  local copies, waits for them, and re-layouts: 1.65 us -> 0.96 us
    pallas_call x1, Pallas kernels: 7.88 us -> 4.83 us  [by_longitude(): pl.pallas_call(lambda *refs: encode_kernel(bands, levels, channels, *refs...]
    pallas_call x1, Pallas kernels: 3.41 us -> 2.26 us  [on_device(): pl.pallas_call(lambda *refs: pack_kernel(bands, levels, *refs), out_shape...]
    reshape x1 -> x0, local copies, waits for them, and re-layouts: 0.69 us -> none  [on_device(): obs_colat.reshape(1, -1)]
where the time goes in v2:
time: 27.5 us; the launch traced here: 27.2 us
  waiting for transfers between devices  10.3 us (37%)
  starting transfers between devices  7.3 us (27%)
  Pallas kernels  7.09 us (26%)
  local copies, waits for them, and re-layouts  0.96 us (3%)
  between operations  0.68 us (2%)
  other arithmetic  0.64 us (2%)
    all_to_all x1, waiting for transfers between devices, on_device(): lax.all_to_all(packed, ('lev', 'band'), split_axis=0, concat_axis=0, tile...  10.3 us
    all_to_all x1, starting transfers between devices, on_device(): lax.all_to_all(packed, ('lev', 'band'), split_axis=0, concat_axis=0, tile...  7.3 us
    pallas_call x1, Pallas kernels, by_longitude(): pl.pallas_call(lambda *refs: encode_kernel(bands, levels, channels, *refs...  4.83 us
    pallas_call x1, Pallas kernels, on_device(): pl.pallas_call(lambda *refs: pack_kernel(bands, levels, *refs), out_shape...  2.26 us
    unnamed x2, local copies, waits for them, and re-layouts  0.96 us
    reduce_max x1, other arithmetic, on_device(): overflow = jnp.max(received[:, channels + 3, :].astype(f32)) > 0.0  0.64 us
  transfers between devices with their start and end apart: 1, of which 1 were waited for; matrix products, arithmetic and copies ran while one was open for 0% of the time, Pallas kernels for 0%

profile of v2, /device:TPU:0, one launch (start us, length us, event | category | flops | bytes accessed | tf_op | source)
XLA Modules:
  0.0 27.2 jit_solution(5646798016742155399)
XLA Ops:
  0.0 2.3 %pack.1 = bf16[32,32,128]{2,1,0:T(8,128)(2,1)} custom-call(s32[1]{0:T(128)} %bitcast.24.refs_0_, s32[1,16]{1,0:T(1,128)} %refs_1_.1, s32[16,128]{1,0:T(8,128)} %bitcast.70, bf16[24,1024]{1,0:T(8,128)(2,1)} %bitcast.69, bf16[8,128]{1,0:T(8,128)(2,1)} %bitcast.64, s32[8,128]{1,0:T(8,128)} %bitcast.63), custom_call_target="tpu_custom_call" | custom-call | tf_op jit(solution)/shard_map/pack/pallas_call | solution.py:308
  2.3 7.3 %all-to-all-start.4 = ((bf16[32,32,128]{2,1,0:T(8,128)(2,1)}), bf16[32,32,128]{2,1,0:T(8,128)(2,1)S(1)}, u32[]{:S(2)}, u32[]{:S(2)}) async-start(bf16[32,32,128]{2,1,0:T(8,128)(2,1)} %pack.1), calls=%async_computation.4 | async-start | bytes 524288 | tf_op jit(solution)/shard_map/all_to_all | solution.py:320
  9.6 10.3 %all-to-all-done.4 = bf16[32,32,128]{2,1,0:T(8,128)(2,1)S(1)} async-done(((bf16[32,32,128]{2,1,0:T(8,128)(2,1)}), bf16[32,32,128]{2,1,0:T(8,128)(2,1)S(1)}, u32[]{:S(2)}, u32[]{:S(2)}) %all-to-all-start.4) | async-done | bytes 262176 | tf_op jit(solution)/shard_map/all_to_all | solution.py:320
  19.9 0.6 %slice_reduce_fusion = bf16[]{:T(256)} fusion(bf16[32,32,128]{2,1,0:T(8,128)(2,1)S(1)} %all-to-all-done.4), kind=kLoop, calls=%fused_computation.78 | loop fusion | flops 4095 | bytes 8194 | tf_op jit(solution)/shard_map/reduce_max | solution.py:321
  21.2 5.1 %conditional.1 = (bf16[128,32,128]{2,1,0:T(8,128)(2,1)S(1)}) conditional(s32[]{:T(128)} %convert_element_type.54, (f32[256]{0:T(256)}, f32[128]{0:T(128)}, bf16[32,32,128]{2,1,0:T(8,128)(2,1)S(1)}, (), bf16[48,256]{1,0:T(8,128)(2,1)}, /*index=5*/bf16[256,128]{1,0:T(8,128)(2,1)}) %tuple.25, (s32[1,16]{1,0:T(1,128)}, s32[1,16,128]{2,1,0:T(8,128)}, ...), branch_computations={%region_1.0_spmd, %region_2.6_spmd} | conditional | flops 612324352 | bytes 12258921 | solution.py:344
  21.2 4.8 %encode.1 = bf16[128,32,128]{2,1,0:T(8,128)(2,1)S(1)} custom-call(bf16[32,32,128]{2,1,0:T(8,128)(2,1)S(1)} %get-tuple-element.125.refs_0_, bf16[128,128]{1,0:T(8,128)(2,1)} %constant.128.clone.1.refs_1_, bf16[48,256]{1,0:T(8,128)(2,1)} %get-tuple-element.127.refs_2_, f32[1,256]{1,0:T(1,128)} %bitcast.76, bf16[256,128]{1,0:T(8,128)(2,1)} %get-tuple-element.129.refs_4_, ...), custom_call_target="tpu_custom_call" | custom-call | tf_op jit(solution)/shard_map/cond/branch_0_fun/encode/pallas_call | solution.py:325
  26.2 0.0 copy-start.2
  26.2 1.0 %copy-done.2 = bf16[128,32,128]{2,1,0:T(8,128)(2,1)} copy-done((bf16[128,32,128]{2,1,0:T(8,128)(2,1)}, bf16[128,32,128]{2,1,0:T(8,128)(2,1)S(1)}, u32[]{:S(2)}) %copy-start.2) | copy-done | bytes 1048600
Async XLA Ops:
  2.3 17.6 %all-to-all-start.4 = ((bf16[32,32,128]{2,1,0:T(8,128)(2,1)}), bf16[32,32,128]{2,1,0:T(8,128)(2,1)S(1)}, u32[]{:S(2)}, u32[]{:S(2)}) async-start(bf16[32,32,128]{2,1,0:T(8,128)(2,1)} %pack.1), calls=%async_computation.4 | async-start | bytes 524288 | tf_op jit(solution)/shard_map/all_to_all | solution.py:320
  26.2 1.0 %copy-start.2 = (bf16[128,32,128]{2,1,0:T(8,128)(2,1)}, bf16[128,32,128]{2,1,0:T(8,128)(2,1)S(1)}, u32[]{:S(2)}) copy-start(bf16[128,32,128]{2,1,0:T(8,128)(2,1)S(1)} %get-tuple-element.296) | copy-start | bytes 3145732

commit v3 on v2

--- a/solution.py
+++ b/solution.py
@@ -132,7 +132,42 @@
     return jnp.concatenate([tiles[i : i + 1] for i in range(tiles.shape[0])], axis=1)
 
 
-def pack_kernel(bands, levels, odd_ref, counts_ref, list_ref, vals_ref, colat_ref, lon_ref, out_ref):
+def whole_copy(array):
+    def kernel(from_ref, to_ref, sem):
+        copy = pltpu.make_async_copy(from_ref, to_ref, sem)
+        copy.start()
+        copy.wait()
+
+    hbm = pl.BlockSpec(memory_space=pltpu.HBM)
+    return pl.pallas_call(
+        kernel,
+        out_shape=jax.ShapeDtypeStruct(array.shape, array.dtype),
+        in_specs=[hbm],
+        out_specs=hbm,
+        scratch_shapes=[pltpu.SemaphoreType.DMA],
+        name="whole_copy",
+    )(array)
+
+
+def pack_kernel(bands, levels, *refs):
+    counts_hbm, list_hbm, lon_hbm, colat_hbm, vals_hbm = refs[:5]
+    out_ref, counts_ref, list_ref, lon_ref, colat_ref, vals_ref, in_sems = refs[5:]
+    loads = [
+        pltpu.make_async_copy(source, target, in_sems.at[i])
+        for i, (source, target) in enumerate(
+            [
+                (counts_hbm, counts_ref),
+                (list_hbm, list_ref),
+                (lon_hbm, lon_ref),
+                (colat_hbm, colat_ref),
+                (vals_hbm, vals_ref),
+            ]
+        )
+    ]
+    for load in loads:
+        load.start()
+    for load in loads:
+        load.wait()
     channels, obs = vals_ref.shape
     blocks = obs // LANES
     low_parts, high_parts = [], []
@@ -149,7 +184,8 @@
     sub_lons = LON_DEV // SUBS
     cap = LANES // SUBS
     groups = bands * SUBS
-    group = (lon // sub_lons) ^ odd_ref[0]
+    odd = lax.axis_index("band") & 1
+    group = (lon // sub_lons) ^ odd
     member = jnp.where(group == iota((groups, obs), 0), 1.0, 0.0)
     earlier = one_where(iota((LANES, LANES), 0) < iota((LANES, LANES), 1))
     carry = jnp.zeros((groups, 1), f32)
@@ -219,8 +255,8 @@
 
 def encode_kernel(
     bands, levels, channels,
-    recv_ref, dct_ref, w_in_ref, b_in_ref, w_out_ref, b_out_ref, out_ref,
-    spread_ref, spec_ref, turn_ref, done_ref, sems,
+    recv_ref, dct_ref, w_in_ref, b_in_ref, w_out_ref, b_out_ref, out_ref, flag_ref,
+    spread_ref, spec_ref, turn_ref, done_ref, mark_ref, sems,
 ):
     modes = LAT_DEV * bands
     feats = levels * channels
@@ -260,7 +296,12 @@
             spread[m * feats : (m + 1) * feats, :] = values * here
         spec_ref[sub] = dot(spread[...], basis, ((1,), (1,))).astype(bf16)
 
-    copies = []
+    flags = recv_ref[0, channels:, :].astype(f32)
+    for source in range(1, levels * bands):
+        flags = jnp.maximum(flags, recv_ref[source, channels:, :].astype(f32))
+    mark_ref[0] = jnp.max(flags[3:4]).astype(jnp.int32)
+    copies = [pltpu.make_async_copy(mark_ref, flag_ref, sems.at[SUBS])]
+    copies[0].start()
     for sub in range(SUBS):
         for first in range(0, sub_lons, batch):
             spectrum = jnp.concatenate(
@@ -303,45 +344,59 @@
     out_rows = w_out.shape[1]
     vmem = pl.BlockSpec(memory_space=pltpu.VMEM)
     smem = pl.BlockSpec(memory_space=pltpu.SMEM)
-    odd = (lax.axis_index("band") & 1).astype(jnp.int32).reshape(1)
-
+
+    hbm = pl.BlockSpec(memory_space=pltpu.HBM)
+    obs = obs_lon.shape[0]
     packed = pl.pallas_call(
         lambda *refs: pack_kernel(bands, levels, *refs),
         out_shape=pltpu.VMEM((levels * bands, ROWS, LANES), bf16),
-        in_specs=[smem, smem, vmem, vmem, vmem, vmem],
+        in_specs=[hbm] * 5,
         out_specs=vmem,
+        scratch_shapes=[
+            pltpu.SMEM((1, bands), jnp.int32),
+            pltpu.VMEM((bands, LANES), jnp.int32),
+            pltpu.VMEM((obs // LANES, LANES), jnp.int32),
+            pltpu.VMEM((obs // LANES, LANES), bf16),
+            pltpu.VMEM((channels, obs), bf16),
+            pltpu.SemaphoreType.DMA((5,)),
+        ],
         compiler_params=pltpu.CompilerParams(vmem_limit_bytes=48 << 20),
         name="pack",
     )(
-        odd, counts, band_list[0], obs_vals[0],
-        obs_colat.reshape(-1, LANES), obs_lon.reshape(-1, LANES),
+        counts, band_list[0], obs_lon.reshape(-1, LANES), obs_colat.reshape(-1, LANES), obs_vals[0],
     )
 
     received = lax.all_to_all(packed, ("lev", "band"), split_axis=0, concat_axis=0, tiled=True)
-    overflow = jnp.max(received[:, channels + 3, :].astype(f32)) > 0.0
-
-    def by_longitude():
-        spread_buffers = SUBS if bands <= 16 else 1
-        return pl.pallas_call(
-            lambda *refs: encode_kernel(bands, levels, channels, *refs),
-            out_shape=jax.ShapeDtypeStruct((out_rows, LON_DEV, modes), bf16),
-            in_specs=[vmem] * 6,
-            out_specs=pl.BlockSpec(memory_space=pltpu.HBM),
-            scratch_shapes=[
-                pltpu.VMEM((spread_buffers, sub_lons * feats, slots), bf16),
-                pltpu.VMEM((SUBS, sub_lons * feats, modes), bf16),
-                pltpu.VMEM((SUBS, modes // LANES, out_rows * sub_lons, LANES), f32),
-                pltpu.VMEM((SUBS, out_rows, sub_lons, modes), bf16),
-                pltpu.SemaphoreType.DMA((SUBS,)),
-            ],
-            compiler_params=pltpu.CompilerParams(vmem_limit_bytes=56 << 20),
-            name="encode",
-        )(received, table_const(modes), w_in, b_in.reshape(1, -1), w_out, b_out.reshape(1, -1))
+    received = pltpu.with_memory_space_constraint(received, pltpu.VMEM)
+    spread_buffers = SUBS if bands <= 16 else 1
+    encoded, overflow = pl.pallas_call(
+        lambda *refs: encode_kernel(bands, levels, channels, *refs),
+        out_shape=[
+            jax.ShapeDtypeStruct((out_rows, LON_DEV, modes), bf16),
+            jax.ShapeDtypeStruct((1,), jnp.int32),
+        ],
+        in_specs=[vmem] * 6,
+        out_specs=[hbm, hbm],
+        scratch_shapes=[
+            pltpu.VMEM((spread_buffers, sub_lons * feats, slots), bf16),
+            pltpu.VMEM((SUBS, sub_lons * feats, modes), bf16),
+            pltpu.VMEM((SUBS, modes // LANES, out_rows * sub_lons, LANES), f32),
+            pltpu.VMEM((SUBS, out_rows, sub_lons, modes), bf16),
+            pltpu.SMEM((1,), jnp.int32),
+            pltpu.SemaphoreType.DMA((SUBS + 1,)),
+        ],
+        compiler_params=pltpu.CompilerParams(vmem_limit_bytes=56 << 20),
+        name="encode",
+    )(received, table_const(modes), w_in, b_in.reshape(1, -1), w_out, b_out.reshape(1, -1))
 
     def by_bands():
-        return by_band(obs_vals, obs_colat, obs_lon, band_list, counts, w_in, b_in, w_out, b_out)
-
-    return lax.cond(overflow, by_bands, by_longitude)
+        vals = whole_copy(obs_vals)
+        return whole_copy(by_band(vals, obs_colat, obs_lon, band_list, counts, w_in, b_in, w_out, b_out))
+
+    def again(carry):
+        return by_bands(), jnp.zeros_like(carry[1])
+
+    return lax.while_loop(lambda carry: carry[1][0] > 0, again, (encoded, overflow))[0]
 
 
 def solution(mesh):

time: 27.5 us -> 25.7 us (0.935)
  blocking collectives: 0 us -> 17.4 us
  waiting for transfers between devices: 10.3 us -> 0 us
  starting transfers between devices: 7.3 us -> 0 us
  local copies, waits for them, and re-layouts: 0.96 us -> 0 us
  other arithmetic: 0.64 us -> 0 us
  loops' own time: 0.24 us -> 0.81 us
  between operations: 0.68 us -> 0.18 us
    all_to_all x0 -> x1, blocking collectives: none -> 17.4 us  [on_device(): lax.all_to_all(packed, ('lev', 'band'), split_axis=0, concat_axis=0, tile...]
    all_to_all x1 -> x0, waiting for transfers between devices: 10.3 us -> none  [on_device(): lax.all_to_all(packed, ('lev', 'band'), split_axis=0, concat_axis=0, tile...]
    all_to_all x1 -> x0, starting transfers between devices: 7.3 us -> none  [on_device(): lax.all_to_all(packed, ('lev', 'band'), split_axis=0, concat_axis=0, tile...]
    unnamed x2 -> x0, local copies, waits for them, and re-layouts: 0.96 us -> none
    reduce_max x1 -> x0, other arithmetic: 0.64 us -> none  [on_device(): overflow = jnp.max(received[:, channels + 3, :].astype(f32)) > 0.0]
    pallas_call x1, Pallas kernels: 2.26 us -> 1.64 us  [on_device(): pl.pallas_call(lambda *refs: pack_kernel(bands, levels, *refs), out_shape...]
    pallas_call x1, Pallas kernels: 4.83 us -> 5.41 us  [on_device(): pl.pallas_call(lambda *refs: encode_kernel(bands, levels, channels, *refs...]
    another operation x1, loops' own time: 0.24 us -> 0.81 us  [on_device(): lax.while_loop(lambda carry: carry[1][0] > 0, again, (encoded, overflow))[0]]
  transfers between devices with their start and end apart: 1 -> 0, of which waited for: 1 -> 0; matrix products, arithmetic and copies ran while one was open for 0% -> 0% of each run, Pallas kernels for 0% -> 0%
where the time goes in v3:
time: 25.7 us; the launch traced here: 25.4 us
  blocking collectives  17.4 us (68%)
  Pallas kernels  7.05 us (27%)
  loops' own time  0.81 us (3%)
    all_to_all x1, blocking collectives, on_device(): lax.all_to_all(packed, ('lev', 'band'), split_axis=0, concat_axis=0, tile...  17.4 us
    pallas_call x1, Pallas kernels, on_device(): pl.pallas_call(lambda *refs: encode_kernel(bands, levels, channels, *refs...  5.41 us
    pallas_call x1, Pallas kernels, on_device(): pl.pallas_call(lambda *refs: pack_kernel(bands, levels, *refs), out_shape...  1.64 us
    another operation x1, loops' own time, on_device(): lax.while_loop(lambda carry: carry[1][0] > 0, again, (encoded, overflow))[0]  0.81 us

profile of v3, /device:TPU:0, one launch (start us, length us, event | category | flops | bytes accessed | tf_op | source)
XLA Modules:
  0.0 25.4 jit_solution(1585042793214573852)
XLA Ops:
  0.0 1.6 %pack.1 = bf16[32,32,128]{2,1,0:T(8,128)(2,1)S(1)} custom-call(s32[1,16]{1,0:T(1,128)} %refs_0_.1, s32[16,128]{1,0:T(8,128)} %bitcast.66, s32[8,128]{1,0:T(8,128)} %bitcast.59, bf16[8,128]{1,0:T(8,128)(2,1)} %bitcast.60, bf16[24,1024]{1,0:T(8,128)(2,1)} %bitcast.68), custom_call_target="tpu_custom_call" | custom-call | tf_op jit(solution)/shard_map/pack/pallas_call | solution.py:350
  1.6 17.4 %all_to_all.24.refs_0_ = bf16[32,32,128]{2,1,0:T(8,128)(2,1)S(1)} all-to-all(bf16[32,32,128]{2,1,0:T(8,128)(2,1)S(1)} %pack.1), channel_id=1, replica_groups=mesh['band'=16,'lev'=2] {'lev','band'}, dimensions={0} | all-to-all | bytes 524288 | tf_op jit(solution)/shard_map/all_to_all | solution.py:369
  19.1 5.4 %encode.1 = (bf16[128,32,128]{2,1,0:T(8,128)(2,1)}, s32[1]{0:T(128)}) custom-call(bf16[32,32,128]{2,1,0:T(8,128)(2,1)S(1)} %all_to_all.24.refs_0_, bf16[128,128]{1,0:T(8,128)(2,1)} %constant.120.clone.refs_1_, bf16[48,256]{1,0:T(8,128)(2,1)} %refs_2_.1, f32[1,256]{1,0:T(1,128)} %bitcast.73, bf16[256,128]{1,0:T(8,128)(2,1)} %refs_4_.1, f32[1,128]{1,0:T(1,128)} %bitcast.72), custom_call_target="tpu_custom_call" | custom-call | tf_op jit(solution)/shard_map/encode/pallas_call | solution.py:372
  24.5 0.8 %while.21 = (bf16[128,32,128]{2,1,0:T(8,128)(2,1)}, s32[1]{0:T(128)}, s32[1,16]{1,0:T(1,128)}, s32[1,16,128]{2,1,0:T(8,128)}, bf16[1,24,1024]{2,1,0:T(8,128)(2,1...) while((bf16[128,32,128]{2,1,0:T(8,128)(2,1)}, ...), condition=%region_4.5_spmd, body=%region_0.4_spmd | while | flops 612324352 | bytes 18550464 | solution.py:399

commit v4 on v3

--- a/solution.py
+++ b/solution.py
@@ -2,8 +2,6 @@
 
 import jax
 import jax.numpy as jnp
-import ml_dtypes
-import numpy as np
 from jax import lax
 from jax.experimental import pallas as pl
 from jax.experimental.pallas import tpu as pltpu
@@ -108,14 +106,6 @@
     return output.astype(jnp.bfloat16)
 
 
-def table_const(length):
-    mode_ids = np.arange(length, dtype=np.float32)[:, None]
-    node_ids = np.arange(length, dtype=np.float32)[None, :]
-    scale = np.where(mode_ids == 0.0, math.sqrt(1.0 / length), math.sqrt(2.0 / length))
-    angle = np.float32(math.pi) * mode_ids * (node_ids + np.float32(0.5)) / np.float32(length)
-    return (scale.astype(np.float32) * np.cos(angle)).astype(ml_dtypes.bfloat16)
-
-
 def dot(lhs, rhs, contract):
     return lax.dot_general(lhs, rhs, (contract, ((), ())), preferred_element_type=f32)
 
@@ -126,6 +116,13 @@
 
 def one_where(mask):
     return jnp.where(mask, 1.0, 0.0).astype(bf16)
+
+
+def cosine_rows(length):
+    mode = iota((length, length), 0)
+    angle = (mode * (2 * iota((length, length), 1) + 1)) & (4 * length - 1)
+    scale = jnp.where(mode == 0, math.sqrt(1.0 / length), math.sqrt(2.0 / length))
+    return (scale * jnp.cos(angle.astype(f32) * (math.pi / (2 * length)))).astype(bf16)
 
 
 def row_of(tiles):
@@ -151,7 +148,8 @@
 
 def pack_kernel(bands, levels, *refs):
     counts_hbm, list_hbm, lon_hbm, colat_hbm, vals_hbm = refs[:5]
-    out_ref, counts_ref, list_ref, lon_ref, colat_ref, vals_ref, in_sems = refs[5:]
+    layers_hbm, out_ref, layers_ref, dct_ref = refs[5:9], refs[9], refs[10:14], refs[14]
+    counts_ref, list_ref, lon_ref, colat_ref, vals_ref, in_sems, layer_sems = refs[15:]
     loads = [
         pltpu.make_async_copy(source, target, in_sems.at[i])
         for i, (source, target) in enumerate(
@@ -164,8 +162,13 @@
             ]
         )
     ]
-    for load in loads:
+    layers = [
+        pltpu.make_async_copy(source, target, layer_sems.at[i])
+        for i, (source, target) in enumerate(zip(layers_hbm, layers_ref))
+    ]
+    for load in loads + layers:
         load.start()
+    dct_ref[...] = cosine_rows(dct_ref.shape[0])
     for load in loads:
         load.wait()
     channels, obs = vals_ref.shape
@@ -231,6 +234,8 @@
         message = jnp.where(flag_row, overflow, message).astype(bf16)
         for level in range(levels):
             out_ref[level * bands + dest] = message
+    for layer in layers:
+        layer.wait()
 
 
 def cheb_rows(colat):
@@ -255,7 +260,7 @@
 
 def encode_kernel(
     bands, levels, channels,
-    recv_ref, dct_ref, w_in_ref, b_in_ref, w_out_ref, b_out_ref, out_ref, flag_ref,
+    recv_ref, w_in_ref, b_in_ref, w_out_ref, b_out_ref, dct_ref, out_ref, flag_ref,
     spread_ref, spec_ref, turn_ref, done_ref, mark_ref, sems,
 ):
     modes = LAT_DEV * bands
@@ -347,11 +352,14 @@
 
     hbm = pl.BlockSpec(memory_space=pltpu.HBM)
     obs = obs_lon.shape[0]
-    packed = pl.pallas_call(
+    layers = [w_in, b_in.reshape(1, -1), w_out, b_out.reshape(1, -1)]
+    packed, *layers = pl.pallas_call(
         lambda *refs: pack_kernel(bands, levels, *refs),
-        out_shape=pltpu.VMEM((levels * bands, ROWS, LANES), bf16),
-        in_specs=[hbm] * 5,
-        out_specs=vmem,
+        out_shape=[pltpu.VMEM((levels * bands, ROWS, LANES), bf16)]
+        + [pltpu.VMEM(layer.shape, layer.dtype) for layer in layers]
+        + [pltpu.VMEM((modes, modes), bf16)],
+        in_specs=[hbm] * 9,
+        out_specs=[vmem] * 6,
         scratch_shapes=[
             pltpu.SMEM((1, bands), jnp.int32),
             pltpu.VMEM((bands, LANES), jnp.int32),
@@ -359,11 +367,13 @@
             pltpu.VMEM((obs // LANES, LANES), bf16),
             pltpu.VMEM((channels, obs), bf16),
             pltpu.SemaphoreType.DMA((5,)),
+            pltpu.SemaphoreType.DMA((4,)),
         ],
-        compiler_params=pltpu.CompilerParams(vmem_limit_bytes=48 << 20),
+        compiler_params=pltpu.CompilerParams(vmem_limit_bytes=(16 if bands <= 16 else 48) << 20),
         name="pack",
     )(
         counts, band_list[0], obs_lon.reshape(-1, LANES), obs_colat.reshape(-1, LANES), obs_vals[0],
+        *layers,
     )
 
     received = lax.all_to_all(packed, ("lev", "band"), split_axis=0, concat_axis=0, tiled=True)
@@ -385,9 +395,9 @@
             pltpu.SMEM((1,), jnp.int32),
             pltpu.SemaphoreType.DMA((SUBS + 1,)),
         ],
-        compiler_params=pltpu.CompilerParams(vmem_limit_bytes=56 << 20),
+        compiler_params=pltpu.CompilerParams(vmem_limit_bytes=(24 if bands <= 16 else 56) << 20),
         name="encode",
-    )(received, table_const(modes), w_in, b_in.reshape(1, -1), w_out, b_out.reshape(1, -1))
+    )(received, *layers)
 
     def by_bands():
         vals = whole_copy(obs_vals)

time: 25.7 us -> 24.9 us (0.969)
  Pallas kernels: 7.05 us -> 6.31 us
    pallas_call x1, Pallas kernels: 5.41 us -> 4.56 us  [on_device(): pl.pallas_call(lambda *refs: encode_kernel(bands, levels, channels, *refs...]
where the time goes in v4:
time: 24.9 us; the launch traced here: 24.7 us
  blocking collectives  17.4 us (70%)
  Pallas kernels  6.31 us (25%)
  loops' own time  0.81 us (3%)
    all_to_all x1, blocking collectives, on_device(): lax.all_to_all(packed, ('lev', 'band'), split_axis=0, concat_axis=0, tile...  17.4 us
    pallas_call x1, Pallas kernels, on_device(): pl.pallas_call(lambda *refs: encode_kernel(bands, levels, channels, *refs...  4.56 us
    pallas_call x1, Pallas kernels, on_device(): pl.pallas_call(lambda *refs: pack_kernel(bands, levels, *refs), out_shape...  1.75 us
    another operation x1, loops' own time, on_device(): lax.while_loop(lambda carry: carry[1][0] > 0, again, (encoded, overflow))[0]  0.81 us

profile of v4, /device:TPU:0, one launch (start us, length us, event | category | flops | bytes accessed | tf_op | source)
XLA Modules:
  0.0 24.7 jit_solution(14029964061089442159)
XLA Ops:
  0.0 1.8 %pack.1 = (bf16[32,32,128]{2,1,0:T(8,128)(2,1)S(1)}, bf16[48,256]{1,0:T(8,128)(2,1)S(1)}, f32[1,256]{1,0:T(1,128)S(1)}, bf16[256,128]{1,0:T(8,128)(2,1)S(1)}, f3...) custom-call(s32[1,16]{1,0:T(1,128)} %refs_0_.1, s32[16,128]{1,0:T(8,128)} %bitcast.66, s32[8,128]{1,0:T(8,128)} %bitcast.59, ...), custom_call_target="tpu_custom_call" | custom-call | tf_op jit(solution)/shard_map/pack/pallas_call | solution.py:356
  1.8 17.4 %all_to_all.24.refs_0_ = bf16[32,32,128]{2,1,0:T(8,128)(2,1)S(1)} all-to-all(bf16[32,32,128]{2,1,0:T(8,128)(2,1)S(1)} %get-tuple-element.162), channel_id=1, replica_groups=mesh['band'=16,'lev'=2] {'lev','band'}, dimensions={0} | all-to-all | bytes 524288 | tf_op jit(solution)/shard_map/all_to_all | solution.py:379
  19.2 4.6 %encode.1 = (bf16[128,32,128]{2,1,0:T(8,128)(2,1)}, s32[1]{0:T(128)}) custom-call(bf16[32,32,128]{2,1,0:T(8,128)(2,1)S(1)} %all_to_all.24.refs_0_, bf16[48,256]{1,0:T(8,128)(2,1)S(1)} %get-tuple-element.163.refs_1_, f32[1,256]{1,0:T(1,128)S(1)} %get-tuple-element.164.refs_2_, bf16[256,128]{1,0:T(8,128)(2,1)S(1)} %get-tuple-element.165.refs_3_, ...), custom_call_target="tpu_custom_call" | custom-call | tf_op jit(solution)/shard_map/encode/pallas_call | solution.py:382
  23.7 0.8 %while.21 = (bf16[128,32,128]{2,1,0:T(8,128)(2,1)}, s32[1]{0:T(128)}, s32[1,16]{1,0:T(1,128)}, s32[1,16,128]{2,1,0:T(8,128)}, bf16[1,24,1024]{2,1,0:T(8,128)(2,1...) while((bf16[128,32,128]{2,1,0:T(8,128)(2,1)}, ...), condition=%region_4.5_spmd, body=%region_0.4_spmd | while | flops 612324352 | bytes 18550464 | solution.py:409

commit v5 on v4

--- a/solution.py
+++ b/solution.py
@@ -305,8 +305,8 @@
     for source in range(1, levels * bands):
         flags = jnp.maximum(flags, recv_ref[source, channels:, :].astype(f32))
     mark_ref[0] = jnp.max(flags[3:4]).astype(jnp.int32)
-    copies = [pltpu.make_async_copy(mark_ref, flag_ref, sems.at[SUBS])]
-    copies[0].start()
+    flag_ref[0] = mark_ref[0]
+    copies = []
     for sub in range(SUBS):
         for first in range(0, sub_lons, batch):
             spectrum = jnp.concatenate(
@@ -383,10 +383,10 @@
         lambda *refs: encode_kernel(bands, levels, channels, *refs),
         out_shape=[
             jax.ShapeDtypeStruct((out_rows, LON_DEV, modes), bf16),
-            jax.ShapeDtypeStruct((1,), jnp.int32),
+            pltpu.SMEM((1,), jnp.int32),
         ],
         in_specs=[vmem] * 6,
-        out_specs=[hbm, hbm],
+        out_specs=[hbm, pl.BlockSpec(memory_space=pltpu.SMEM)],
         scratch_shapes=[
             pltpu.VMEM((spread_buffers, sub_lons * feats, slots), bf16),
             pltpu.VMEM((SUBS, sub_lons * feats, modes), bf16),
@@ -406,7 +406,7 @@
     def again(carry):
         return by_bands(), jnp.zeros_like(carry[1])
 
-    return lax.while_loop(lambda carry: carry[1][0] > 0, again, (encoded, overflow))[0]
+    return lax.while_loop(lambda carry: carry[1], again, (encoded, overflow[0] > 0))[0]
 
 
 def solution(mesh):

time: 24.9 us -> 24.2 us (0.972)
  loops' own time: 0.81 us -> 0.19 us
    another operation x1, loops' own time: 0.81 us -> 0.19 us  [on_device(): lax.while_loop(lambda carry: carry[1], again, (encoded, overflow[0] > 0))[0]]
where the time goes in v5:
time: 24.2 us; the launch traced here: 24.1 us
  blocking collectives  17.4 us (72%)
  Pallas kernels  6.29 us (26%)
    all_to_all x1, blocking collectives, on_device(): lax.all_to_all(packed, ('lev', 'band'), split_axis=0, concat_axis=0, tile...  17.4 us
    pallas_call x1, Pallas kernels, on_device(): pl.pallas_call(lambda *refs: encode_kernel(bands, levels, channels, *refs...  4.54 us
    pallas_call x1, Pallas kernels, on_device(): pl.pallas_call(lambda *refs: pack_kernel(bands, levels, *refs), out_shape...  1.75 us

profile of v5, /device:TPU:0, one launch (start us, length us, event | category | flops | bytes accessed | tf_op | source)
XLA Modules:
  0.0 24.1 jit_solution(14264361737757625357)
XLA Ops:
  0.0 1.8 %pack.1 = (bf16[32,32,128]{2,1,0:T(8,128)(2,1)S(1)}, bf16[48,256]{1,0:T(8,128)(2,1)S(1)}, f32[1,256]{1,0:T(1,128)S(1)}, bf16[256,128]{1,0:T(8,128)(2,1)S(1)}, f3...) custom-call(s32[1,16]{1,0:T(1,128)} %refs_0_.1, s32[16,128]{1,0:T(8,128)} %bitcast.66, s32[8,128]{1,0:T(8,128)} %bitcast.59, ...), custom_call_target="tpu_custom_call" | custom-call | tf_op jit(solution)/shard_map/pack/pallas_call | solution.py:356
  1.8 17.4 %all_to_all.24.refs_0_ = bf16[32,32,128]{2,1,0:T(8,128)(2,1)S(1)} all-to-all(bf16[32,32,128]{2,1,0:T(8,128)(2,1)S(1)} %get-tuple-element.162), channel_id=1, replica_groups=mesh['band'=16,'lev'=2] {'lev','band'}, dimensions={0} | all-to-all | bytes 524288 | tf_op jit(solution)/shard_map/all_to_all | solution.py:379
  19.2 4.5 %encode.1 = (bf16[128,32,128]{2,1,0:T(8,128)(2,1)}, s32[1]{0:T(128)S(4)}) custom-call(bf16[32,32,128]{2,1,0:T(8,128)(2,1)S(1)} %all_to_all.24.refs_0_, bf16[48,256]{1,0:T(8,128)(2,1)S(1)} %get-tuple-element.163.refs_1_, f32[1,256]{1,0:T(1,128)S(1)} %get-tuple-element.164.refs_2_, bf16[256,128]{1,0:T(8,128)(2,1)S(1)} %get-tuple-element.165.refs_3_, ...), custom_call_target="tpu_custom_call" | custom-call | tf_op jit(solution)/shard_map/encode/pallas_call | solution.py:382
  23.7 0.2 while.21

commit v6 on v5

--- a/solution.py
+++ b/solution.py
@@ -10,7 +10,9 @@
 LAT_DEV = 8
 LON_DEV = 32
 SUBS = 2
-ROWS = 32
+SPARE = 4
+FIELD_ROWS = 16
+FIELDS = 3
 LANES = 128
 
 norm_eps = 1e-05
@@ -123,6 +125,16 @@
     angle = (mode * (2 * iota((length, length), 1) + 1)) & (4 * length - 1)
     scale = jnp.where(mode == 0, math.sqrt(1.0 / length), math.sqrt(2.0 / length))
     return (scale * jnp.cos(angle.astype(f32) * (math.pi / (2 * length)))).astype(bf16)
+
+
+def spare_lanes():
+    half = LANES // SUBS
+    source, target = iota((LANES, LANES), 0), iota((LANES, LANES), 1)
+    return one_where(
+        ((source & (half - 1)) >= half - SPARE)
+        & (source // half == target // half)
+        & ((source & (SPARE - 1)) == (target & (SPARE - 1)))
+    )
 
 
 def row_of(tiles):
@@ -185,7 +197,7 @@
 
     lon = row_of(lon_ref[...])
     sub_lons = LON_DEV // SUBS
-    cap = LANES // SUBS
+    cap = LANES // SUBS - SPARE
     groups = bands * SUBS
     odd = lax.axis_index("band") & 1
     group = (lon // sub_lons) ^ odd
@@ -200,7 +212,7 @@
         carry = carry + jnp.sum(part, axis=1, keepdims=True)
     place = jnp.concatenate(places, axis=1).astype(jnp.int32)
     overflow = jnp.where(jnp.max(carry) > cap, 1.0, 0.0)
-    slot = jnp.where(place < cap, group * cap + place, -1)
+    slot = jnp.where(place < cap, group * (LANES // SUBS) + place, -1)
 
     depth = 2 * LANES
     chunks = obs // depth
@@ -212,28 +224,38 @@
     found = dot(jnp.concatenate([held, chunk], axis=0).astype(bf16), lane, ((1,), (1,)))
     held, chunk = row_of(found[:bands]), row_of(found[bands:])
 
+    row_count = -(-(channels + FIELDS) // 16) * 16
     rows = jnp.concatenate(
         [
             vals_ref[...].astype(f32),
             (lon & (LON_DEV - 1)).astype(f32),
             band_row,
             row_of(colat_ref[...].astype(f32)),
-            jnp.zeros((ROWS - channels - 3, obs), f32),
+            jnp.zeros((row_count - channels - FIELDS, obs), f32),
         ],
         axis=0,
     ).astype(bf16)
     stacked = jnp.concatenate([rows[:, i * depth : (i + 1) * depth] for i in range(chunks)], axis=0)
     pick = one_where(held == (iota((depth, bands * LANES), 0) + 1).astype(f32))
     picked = dot(stacked, pick, ((1,), (0,)))
-    messages = jnp.zeros((ROWS, bands * LANES), f32)
+    found = jnp.zeros((row_count, bands * LANES), f32)
     for i in range(chunks):
-        messages = jnp.where(chunk == float(i), picked[i * ROWS : (i + 1) * ROWS], messages)
-    flag_row = iota((ROWS, LANES), 0) == channels + 3
+        found = jnp.where(chunk == float(i), picked[i * row_count : (i + 1) * row_count], found)
+
+    half_lane = iota((channels, bands * LANES), 1) & (LANES // SUBS - 1)
+    row = iota((channels, bands * LANES), 0) + lax.axis_index("lev") * channels
+    lon_row, band_row, colat_row = (found[channels + i : channels + i + 1] for i in range(FIELDS))
+    lon_row = jnp.where(half_lane[:1] >= cap, overflow, lon_row)
+    field = jnp.where(row < FIELD_ROWS, lon_row, jnp.where(row < 2 * FIELD_ROWS, band_row, colat_row))
+    wanted = (half_lane // SPARE == (row & (FIELD_ROWS - 1))) & (row < FIELDS * FIELD_ROWS)
+    field = jnp.where(wanted, field, 0.0)
+    tiles = [slice(dest * LANES, (dest + 1) * LANES) for dest in range(bands)]
+    field = jnp.concatenate([field[:, tile] for tile in tiles], axis=0).astype(bf16)
+    field = dot(field, spare_lanes(), ((1,), (1,)))
     for dest in range(bands):
-        message = messages[:, dest * LANES : (dest + 1) * LANES]
-        message = jnp.where(flag_row, overflow, message).astype(bf16)
+        message = found[:channels, tiles[dest]] + field[dest * channels : (dest + 1) * channels]
         for level in range(levels):
-            out_ref[level * bands + dest] = message
+            out_ref[level * bands + dest] = message.astype(bf16)
     for layer in layers:
         layer.wait()
 
@@ -261,12 +283,12 @@
 def encode_kernel(
     bands, levels, channels,
     recv_ref, w_in_ref, b_in_ref, w_out_ref, b_out_ref, dct_ref, out_ref, flag_ref,
-    spread_ref, spec_ref, turn_ref, done_ref, mark_ref, sems,
+    spread_ref, spec_ref, turn_ref, done_ref, sems,
 ):
     modes = LAT_DEV * bands
     feats = levels * channels
     sub_lons = LON_DEV // SUBS
-    lower = iota((ROWS, LANES), 1) < LANES // SUBS
+    lower = iota((channels, LANES), 1) < LANES // SUBS
     w_first = w_in_ref[...].astype(f32).T.astype(bf16)
     w_second = w_out_ref[...].astype(f32).T.astype(bf16)
     out_rows = w_second.shape[0]
@@ -285,11 +307,32 @@
             pieces.append(jnp.where(lower, even, odd) if sub == 0 else jnp.where(lower, odd, even))
         return jnp.concatenate(pieces, axis=1)
 
+    slots = bands * LANES // SUBS
+    carriers = -(-FIELDS * FIELD_ROWS // channels)
+    half_lane = iota((FIELD_ROWS, slots), 1) & (LANES // SUBS - 1)
+    wanted = half_lane // SPARE == iota((FIELD_ROWS, slots), 0)
+    unused = half_lane[:1] >= LANES // SUBS - SPARE
+    flags = []
     for sub in range(SUBS):
         parts = [half(level, sub) for level in range(levels)]
-        meta = parts[0][channels:].astype(f32)
-        values = jnp.concatenate([part[:channels] for part in parts], axis=0)
-        lon, band, colat = meta[0:1], meta[1:2], meta[2:3]
+        values = jnp.concatenate(parts, axis=0)
+        wide = jnp.concatenate([part.astype(f32) for part in parts[:carriers]], axis=0)
+        wide = wide[: FIELDS * FIELD_ROWS]
+        tiles = [wide[:, i * LANES : (i + 1) * LANES] for i in range(slots // LANES)]
+        fields = dot(jnp.concatenate(tiles, axis=0).astype(bf16), spare_lanes(), ((1,), (0,)))
+        fields = jnp.concatenate(
+            [fields[i * wide.shape[0] : (i + 1) * wide.shape[0]] for i in range(len(tiles))], axis=1
+        )
+        lon, band, colat = (
+            jnp.sum(
+                jnp.where(wanted, fields[i * FIELD_ROWS : (i + 1) * FIELD_ROWS], 0.0),
+                axis=0,
+                keepdims=True,
+            )
+            for i in range(FIELDS)
+        )
+        flags.append(jnp.where(unused, lon, 0.0))
+        lon = jnp.where(unused, -1.0, lon)
         weight = cheb_rows(colat)
         nodes = jnp.concatenate(
             [jnp.where(band == float(b), weight, 0.0) for b in range(bands)], axis=0
@@ -301,11 +344,7 @@
             spread[m * feats : (m + 1) * feats, :] = values * here
         spec_ref[sub] = dot(spread[...], basis, ((1,), (1,))).astype(bf16)
 
-    flags = recv_ref[0, channels:, :].astype(f32)
-    for source in range(1, levels * bands):
-        flags = jnp.maximum(flags, recv_ref[source, channels:, :].astype(f32))
-    mark_ref[0] = jnp.max(flags[3:4]).astype(jnp.int32)
-    flag_ref[0] = mark_ref[0]
+    flag_ref[0] = jnp.max(jnp.maximum(*flags)).astype(jnp.int32)
     copies = []
     for sub in range(SUBS):
         for first in range(0, sub_lons, batch):
@@ -355,7 +394,7 @@
     layers = [w_in, b_in.reshape(1, -1), w_out, b_out.reshape(1, -1)]
     packed, *layers = pl.pallas_call(
         lambda *refs: pack_kernel(bands, levels, *refs),
-        out_shape=[pltpu.VMEM((levels * bands, ROWS, LANES), bf16)]
+        out_shape=[pltpu.VMEM((levels * bands, channels, LANES), bf16)]
         + [pltpu.VMEM(layer.shape, layer.dtype) for layer in layers]
         + [pltpu.VMEM((modes, modes), bf16)],
         in_specs=[hbm] * 9,
@@ -392,8 +431,7 @@
             pltpu.VMEM((SUBS, sub_lons * feats, modes), bf16),
             pltpu.VMEM((SUBS, modes // LANES, out_rows * sub_lons, LANES), f32),
             pltpu.VMEM((SUBS, out_rows, sub_lons, modes), bf16),
-            pltpu.SMEM((1,), jnp.int32),
-            pltpu.SemaphoreType.DMA((SUBS + 1,)),
+            pltpu.SemaphoreType.DMA((SUBS,)),
         ],
         compiler_params=pltpu.CompilerParams(vmem_limit_bytes=(24 if bands <= 16 else 56) << 20),
         name="encode",

time: 24.2 us -> 23.2 us (0.959)
  blocking collectives: 17.4 us -> 16 us
    all_to_all x1, blocking collectives: 17.4 us -> 16 us  [on_device(): lax.all_to_all(packed, ('lev', 'band'), split_axis=0, concat_axis=0, tile...]
where the time goes in v6:
time: 23.2 us; the launch traced here: 22.8 us
  blocking collectives  16 us (69%)
  Pallas kernels  6.44 us (28%)
    all_to_all x1, blocking collectives, on_device(): lax.all_to_all(packed, ('lev', 'band'), split_axis=0, concat_axis=0, tile...  16 us
    pallas_call x1, Pallas kernels, on_device(): pl.pallas_call(lambda *refs: encode_kernel(bands, levels, channels, *refs...  4.56 us
    pallas_call x1, Pallas kernels, on_device(): pl.pallas_call(lambda *refs: pack_kernel(bands, levels, *refs), out_shape...  1.89 us

profile of v6, /device:TPU:0, one launch (start us, length us, event | category | flops | bytes accessed | tf_op | source)
XLA Modules:
  0.0 22.8 jit_solution(12816848525721674084)
XLA Ops:
  0.0 1.9 %pack.1 = (bf16[32,24,128]{2,1,0:T(8,128)(2,1)S(1)}, bf16[48,256]{1,0:T(8,128)(2,1)S(1)}, f32[1,256]{1,0:T(1,128)S(1)}, bf16[256,128]{1,0:T(8,128)(2,1)S(1)}, f3...) custom-call(s32[1,16]{1,0:T(1,128)} %refs_0_.1, s32[16,128]{1,0:T(8,128)} %bitcast.66, s32[8,128]{1,0:T(8,128)} %bitcast.59, ...), custom_call_target="tpu_custom_call" | custom-call | tf_op jit(solution)/shard_map/pack/pallas_call | solution.py:395
  1.9 16.0 %all_to_all.24.refs_0_ = bf16[32,24,128]{2,1,0:T(8,128)(2,1)S(1)} all-to-all(bf16[32,24,128]{2,1,0:T(8,128)(2,1)S(1)} %get-tuple-element.162), channel_id=1, replica_groups=mesh['band'=16,'lev'=2] {'lev','band'}, dimensions={0} | all-to-all | bytes 393216 | tf_op jit(solution)/shard_map/all_to_all | solution.py:418
  17.9 4.6 %encode.1 = (bf16[128,32,128]{2,1,0:T(8,128)(2,1)}, s32[1]{0:T(128)S(4)}) custom-call(bf16[32,24,128]{2,1,0:T(8,128)(2,1)S(1)} %all_to_all.24.refs_0_, bf16[48,256]{1,0:T(8,128)(2,1)S(1)} %get-tuple-element.163.refs_1_, f32[1,256]{1,0:T(1,128)S(1)} %get-tuple-element.164.refs_2_, bf16[256,128]{1,0:T(8,128)(2,1)S(1)} %get-tuple-element.165.refs_3_, ...), custom_call_target="tpu_custom_call" | custom-call | tf_op jit(solution)/shard_map/encode/pallas_call | solution.py:421
  22.5 0.2 while.21

commit v7 on v6

--- a/solution.py
+++ b/solution.py
@@ -181,7 +181,7 @@
     for load in loads + layers:
         load.start()
     dct_ref[...] = cosine_rows(dct_ref.shape[0])
-    for load in loads:
+    for load in loads[:3]:
         load.wait()
     channels, obs = vals_ref.shape
     blocks = obs // LANES
@@ -225,6 +225,8 @@
     held, chunk = row_of(found[:bands]), row_of(found[bands:])
 
     row_count = -(-(channels + FIELDS) // 16) * 16
+    for load in loads[3:]:
+        load.wait()
     rows = jnp.concatenate(
         [
             vals_ref[...].astype(f32),
@@ -274,10 +276,9 @@
     return total
 
 
-def gelu(x):
+def gelu_of_twice(half):
     slope = math.sqrt(2.0 / math.pi)
-    half = 0.5 * x
-    return half + half * jnp.tanh(x * (slope + (0.044715 * slope) * (x * x)))
+    return half + half * jnp.tanh(half * (2.0 * slope + (8.0 * 0.044715 * slope) * (half * half)))
 
 
 def encode_kernel(
@@ -294,7 +295,7 @@
     out_rows = w_second.shape[0]
     batch = max(1, sub_lons * LANES // modes)
     lane_tiles = batch * modes // LANES
-    b_first = jnp.broadcast_to(b_in_ref[...], (LANES, b_in_ref.shape[1])).T
+    b_first = jnp.broadcast_to(0.5 * b_in_ref[...], (LANES, b_in_ref.shape[1])).T
     b_second = jnp.broadcast_to(b_out_ref[...], (LANES, b_out_ref.shape[1])).T
     b_first = jnp.concatenate([b_first] * lane_tiles, axis=1)
     b_second = jnp.concatenate([b_second] * lane_tiles, axis=1)
@@ -357,7 +358,7 @@
                 jnp.sum(wide * wide, axis=0, keepdims=True) * (1.0 / feats) + norm_eps
             )
             pre_act = dot(w_first, spectrum, ((1,), (0,)))
-            hidden = gelu(pre_act * inv_norm + b_first).astype(bf16)
+            hidden = gelu_of_twice(pre_act * (0.5 * inv_norm) + b_first).astype(bf16)
             encoded = dot(w_second, hidden, ((1,), (0,))) + b_second
             for j in range(batch):
                 for i in range(modes // LANES):

time: 23.2 us -> 22.9 us (0.987)
  Pallas kernels: 6.44 us -> 6.18 us
where the time goes in v7:
time: 22.9 us; the launch traced here: 22.6 us
  blocking collectives  16 us (70%)
  Pallas kernels  6.18 us (27%)
    all_to_all x1, blocking collectives, on_device(): lax.all_to_all(packed, ('lev', 'band'), split_axis=0, concat_axis=0, tile...  16 us
    pallas_call x1, Pallas kernels, on_device(): pl.pallas_call(lambda *refs: encode_kernel(bands, levels, channels, *refs...  4.48 us
    pallas_call x1, Pallas kernels, on_device(): pl.pallas_call(lambda *refs: pack_kernel(bands, levels, *refs), out_shape...  1.7 us

profile of v7, /device:TPU:0, one launch (start us, length us, event | category | flops | bytes accessed | tf_op | source)
XLA Modules:
  0.0 22.6 jit_solution(9104271711596916691)
XLA Ops:
  0.0 1.7 %pack.1 = (bf16[32,24,128]{2,1,0:T(8,128)(2,1)S(1)}, bf16[48,256]{1,0:T(8,128)(2,1)S(1)}, f32[1,256]{1,0:T(1,128)S(1)}, bf16[256,128]{1,0:T(8,128)(2,1)S(1)}, f3...) custom-call(s32[1,16]{1,0:T(1,128)} %refs_0_.1, s32[16,128]{1,0:T(8,128)} %bitcast.66, s32[8,128]{1,0:T(8,128)} %bitcast.59, ...), custom_call_target="tpu_custom_call" | custom-call | tf_op jit(solution)/shard_map/pack/pallas_call | solution.py:396
  1.7 16.0 %all_to_all.24.refs_0_ = bf16[32,24,128]{2,1,0:T(8,128)(2,1)S(1)} all-to-all(bf16[32,24,128]{2,1,0:T(8,128)(2,1)S(1)} %get-tuple-element.162), channel_id=1, replica_groups=mesh['band'=16,'lev'=2] {'lev','band'}, dimensions={0} | all-to-all | bytes 393216 | tf_op jit(solution)/shard_map/all_to_all | solution.py:419
  17.7 4.5 %encode.1 = (bf16[128,32,128]{2,1,0:T(8,128)(2,1)}, s32[1]{0:T(128)S(4)}) custom-call(bf16[32,24,128]{2,1,0:T(8,128)(2,1)S(1)} %all_to_all.24.refs_0_, bf16[48,256]{1,0:T(8,128)(2,1)S(1)} %get-tuple-element.163.refs_1_, f32[1,256]{1,0:T(1,128)S(1)} %get-tuple-element.164.refs_2_, bf16[256,128]{1,0:T(8,128)(2,1)S(1)} %get-tuple-element.165.refs_3_, ...), custom_call_target="tpu_custom_call" | custom-call | tf_op jit(solution)/shard_map/encode/pallas_call | solution.py:422
  22.2 0.2 while.21
